TPU v7x, 128 devices: a whole 4x4x4 slice. The times are simulated.
128 devices in a mesh: dp: 8 (over y_lo, z), ctx: 16 (over y_hi, x, core).
Axes of the slice: x: 4, y: 4 (y_hi: 2, y_lo: 2; y = y_hi * 2 + y_lo), z: 4, core: 2. Of those that a mesh axis runs over, the one named last changes fastest.
Arguments:
- tokens: bfloat16 [16384, 768], P(('dp', 'ctx')), may hold values from -6 to 6
- cotangent: bfloat16 [16384, 768], P(('dp', 'ctx')), may hold values from -6 to 6
- w_qkv: bfloat16 [2, 768, 2304], P(None, 'dp'), may hold values from -0.21875 to 0.21875
- w_out: bfloat16 [2, 768, 768], P(None, 'dp'), may hold values from -0.875 to 0.875
- w_up: bfloat16 [2, 768, 3072], P(None, 'dp'), may hold values from -0.21875 to 0.21875
- w_down: bfloat16 [2, 3072, 768], P(None, 'dp'), may hold values from -0.109375 to 0.109375
- gains: bfloat16 [2, 2, 768], P(None, None, 'dp'), may hold values from 0.099609375 to 1.8984375
- shifts: bfloat16 [2, 6, 768], P(None, None, 'dp'), may hold values from -3 to 3
- up_bias: bfloat16 [2, 3072], P(None, 'dp'), may hold values from -3 to 3
Outputs:
- output: bfloat16 [16384, 768], P(('dp', 'ctx'))
- grad_tokens: float32 [16384, 768], P(('dp', 'ctx'))
- grad_qkv: float32 [2, 768, 2304], P(None, 'dp')
- grad_out: float32 [2, 768, 768], P(None, 'dp')
- grad_up: float32 [2, 768, 3072], P(None, 'dp')
- grad_down: float32 [2, 3072, 768], P(None, 'dp')
- grad_gains: float32 [2, 2, 768], P(None, None, 'dp')
- grad_shifts: float32 [2, 6, 768], P(None, None, 'dp')
- grad_upbias: float32 [2, 3072], P(None, 'dp')
All inputs are finite; a program needn't handle non-finite values.
Results may differ from a plain program's by a relative error of at most 0.023.
Values may be sent and summed in bfloat16 or wider, within the bound.
No kernel may reach another device: no remote copies, remote signals or barrier semaphores. Data moves between devices by JAX's collectives and lax.ppermute only.
A program may use at most 192 MiB of HBM per device.

v0:
```python
import jax
import jax.numpy as jnp
from jax import lax
from jax.sharding import PartitionSpec as P

HEADS = 12
HEAD = 64
LAYERS = 2


EPSILON = 1e-05
NEGATIVE = -1e30


def sent_together(arrays, axis, dim, along):
    widths = [a.shape[along] for a in arrays]
    both = jnp.concatenate(arrays, axis=along)
    filled = lax.all_gather(both, axis, axis=dim, tiled=True)
    return tuple(jnp.split(filled, [sum(widths[:k]) for k in range(1, len(widths))], axis=along))


def in_one_piece(arrays, axis, dim, along):
    ends, at = ([], 0)
    for a in arrays[:-1]:
        at += a.shape[along]
        ends.append(at)
    both = jnp.concatenate(arrays, axis=along)
    return tuple(
        jnp.split(lax.psum_scatter(both, axis, scatter_dimension=dim, tiled=True), ends, axis=along)
    )


def normalize(values, gain, shift):
    average = jnp.mean(values, axis=-1, keepdims=True)
    centered = values - average
    spread = jnp.mean(centered * centered, axis=-1, keepdims=True)
    return centered * lax.rsqrt(spread + EPSILON) * gain + shift


def matmul(left, right):
    return jnp.dot(left, right, preferred_element_type=jnp.float32)


def contract_rows(left, right):
    return lax.dot_general(
        left, right, (((0,), (0,)), ((), ())), preferred_element_type=jnp.float32
    )


def contract_features(left, right):
    return lax.dot_general(
        left, right, (((1,), (1,)), ((), ())), preferred_element_type=jnp.float32
    )


def attend(queries, keys, values, position):
    rows, width = queries.shape
    query_heads = queries.reshape(rows, HEADS, HEAD)
    query_pos = position + jnp.arange(rows, dtype=jnp.int32)
    peak = jnp.full((HEADS, rows), NEGATIVE, jnp.float32)
    key_piece, value_piece = sent_together((keys, values), "ctx", 0, 1)
    count = key_piece.shape[0]
    key_heads = key_piece.reshape(count, HEADS, HEAD)
    value_heads = value_piece.reshape(count, HEADS, HEAD)
    scores = jnp.einsum("qhd,khd->hqk", query_heads, key_heads, preferred_element_type=jnp.float32)
    allowed = jnp.arange(count, dtype=jnp.int32)[None, :] <= query_pos[:, None]
    masked = jnp.where(allowed[None], scores, NEGATIVE)
    new_peak = jnp.maximum(peak, jnp.max(masked, axis=2))
    weights = jnp.where(allowed[None], jnp.exp(masked - new_peak[..., None]), 0.0)
    total = jnp.sum(weights, axis=2)
    accum = jnp.einsum(
        "hqk,khd->hqd",
        weights.astype(jnp.bfloat16),
        value_heads,
        preferred_element_type=jnp.float32,
    )
    peak, total, accum = (new_peak, total, accum)
    context = (accum / total[..., None]).transpose(1, 0, 2).reshape(rows, width)
    logsum = peak + jnp.log(total)
    return (context, logsum)


def score_block(query_heads, grad_heads, key_heads, value_heads, query_pos, key_pos, logsum, delta):
    scores = jnp.einsum("qhd,khd->hqk", query_heads, key_heads, preferred_element_type=jnp.float32)
    allowed = key_pos[None, :] <= query_pos[:, None]
    probs = jnp.where(allowed[None], jnp.exp(scores - logsum[..., None]), 0.0)
    grad_probs = jnp.einsum(
        "qhd,khd->hqk", grad_heads, value_heads, preferred_element_type=jnp.float32
    )
    grad_scores = (probs * (grad_probs - delta[..., None])).astype(jnp.bfloat16)
    return (probs.astype(jnp.bfloat16), grad_scores)


def attend_back(
    queries, keys, values, keys_all, values_all, context, logsum, grad_context, position
):
    rows, width = queries.shape
    seq_len = keys_all.shape[0]
    key_block = min(512, seq_len)
    query_heads = queries.reshape(rows, HEADS, HEAD)
    grad_heads = grad_context.reshape(rows, HEADS, HEAD)
    delta = jnp.sum(grad_heads.astype(jnp.float32) * context.reshape(rows, HEADS, HEAD), axis=2).T
    query_pos = position + jnp.arange(rows, dtype=jnp.int32)
    count = (position + rows + key_block - 1) // key_block

    def visit_query(block, grad_query):
        start = block * key_block
        key_piece = lax.dynamic_slice_in_dim(keys_all, start, key_block, 0).reshape(
            key_block, HEADS, HEAD
        )
        value_piece = lax.dynamic_slice_in_dim(values_all, start, key_block, 0).reshape(
            key_block, HEADS, HEAD
        )
        key_pos = start + jnp.arange(key_block, dtype=jnp.int32)
        probs_low, grad_scores = score_block(
            query_heads, grad_heads, key_piece, value_piece, query_pos, key_pos, logsum, delta
        )
        return grad_query + jnp.einsum(
            "hqk,khd->qhd", grad_scores, key_piece, preferred_element_type=jnp.float32
        )

    grad_query = lax.fori_loop(0, count, visit_query, jnp.zeros((rows, HEADS, HEAD), jnp.float32))
    all_queries, all_grads = sent_together((queries, grad_context), "ctx", 0, 1)
    all_logsum, all_delta = sent_together((logsum, delta), "ctx", 1, 0)
    own_keys = keys.reshape(rows, HEADS, HEAD)
    own_values = values.reshape(rows, HEADS, HEAD)
    first = position // key_block
    last = seq_len // key_block

    def visit_keys(block, carry):
        grad_keys, grad_values = carry
        start = block * key_block
        query_piece = lax.dynamic_slice_in_dim(all_queries, start, key_block, 0).reshape(
            key_block, HEADS, HEAD
        )
        grad_piece = lax.dynamic_slice_in_dim(all_grads, start, key_block, 0).reshape(
            key_block, HEADS, HEAD
        )
        lse_piece = lax.dynamic_slice_in_dim(all_logsum, start, key_block, 1)
        delta_piece = lax.dynamic_slice_in_dim(all_delta, start, key_block, 1)
        piece_pos = start + jnp.arange(key_block, dtype=jnp.int32)
        probs_low, grad_scores = score_block(
            query_piece,
            grad_piece,
            own_keys,
            own_values,
            piece_pos,
            query_pos,
            lse_piece,
            delta_piece,
        )
        grad_values = grad_values + jnp.einsum(
            "hqk,qhd->khd", probs_low, grad_piece, preferred_element_type=jnp.float32
        )
        grad_keys = grad_keys + jnp.einsum(
            "hqk,qhd->khd", grad_scores, query_piece, preferred_element_type=jnp.float32
        )
        return (grad_keys, grad_values)

    zeros_kv = jnp.zeros((rows, HEADS, HEAD), jnp.float32)
    grad_keys, grad_values = lax.fori_loop(first, last, visit_keys, (zeros_kv, zeros_kv))
    return (
        grad_query.reshape(rows, width),
        grad_keys.reshape(rows, width),
        grad_values.reshape(rows, width),
    )


def layer_forward(state, weights, position):
    w_qkv, w_out, w_up, w_down, gains, shifts, up_bias = weights
    gains = gains.astype(jnp.float32)
    shifts = shifts.astype(jnp.float32)
    width = state.shape[1]
    normed = normalize(state, gains[0], shifts[0]).astype(jnp.bfloat16)
    bias_full = jnp.concatenate([shifts[2], jnp.zeros_like(shifts[2]), shifts[3]])
    mixed = matmul(normed, w_qkv) + bias_full
    queries = (mixed[:, :width] * HEAD ** (-0.5)).astype(jnp.bfloat16)
    keys = mixed[:, width : 2 * width].astype(jnp.bfloat16)
    values = mixed[:, 2 * width :].astype(jnp.bfloat16)
    context, logsum = attend(queries, keys, values, position)
    attended = context.astype(jnp.bfloat16)
    middle = state + (matmul(attended, w_out) + shifts[4])
    normed_two = normalize(middle, gains[1], shifts[1]).astype(jnp.bfloat16)
    upper = matmul(normed_two, w_up) + up_bias.astype(jnp.float32)
    active = jax.nn.gelu(upper).astype(jnp.bfloat16)
    result = middle + (matmul(active, w_down) + shifts[5])
    kept = (
        state,
        normed,
        queries,
        keys,
        values,
        context,
        logsum,
        attended,
        middle,
        normed_two,
        upper,
        active,
    )
    return (result, kept)


def layer_backward(kept, weights, grad_result, position):
    (
        state,
        normed,
        queries,
        keys,
        values,
        context,
        logsum,
        attended,
        middle,
        normed_two,
        upper,
        active,
    ) = kept
    w_qkv, w_out, w_up, w_down, gains, shifts, up_bias = weights
    gains = gains.astype(jnp.float32)
    shifts = shifts.astype(jnp.float32)
    width = state.shape[1]
    grad_branch_two = grad_result.astype(jnp.bfloat16)
    grad_down = contract_rows(active, grad_branch_two)
    down_bias = jnp.sum(grad_branch_two.astype(jnp.float32), axis=0)
    grad_active = contract_features(grad_branch_two, w_down)
    unused, gelu_back = jax.vjp(jax.nn.gelu, upper)
    grad_upper = gelu_back(grad_active)[0].astype(jnp.bfloat16)
    grad_up = contract_rows(normed_two, grad_upper)
    grad_upbias = jnp.sum(grad_upper.astype(jnp.float32), axis=0)
    grad_normed_two = contract_features(grad_upper, w_up)
    unused, norm_back_two = jax.vjp(normalize, middle, gains[1], shifts[1])
    grad_mid_part, gain_two, shift_two = norm_back_two(grad_normed_two)
    grad_middle = grad_result + grad_mid_part
    grad_branch = grad_middle.astype(jnp.bfloat16)
    grad_out = contract_rows(attended, grad_branch)
    out_bias = jnp.sum(grad_branch.astype(jnp.float32), axis=0)
    grad_context = contract_features(grad_branch, w_out).astype(jnp.bfloat16)
    keys_all, values_all = sent_together((keys, values), "ctx", 0, 1)
    grad_query, grad_keys, grad_values = attend_back(
        queries, keys, values, keys_all, values_all, context, logsum, grad_context, position
    )
    grad_mixed = jnp.concatenate(
        [grad_query * HEAD ** (-0.5), grad_keys, grad_values], axis=1
    ).astype(jnp.bfloat16)
    grad_qkv = contract_rows(normed, grad_mixed)
    column_sums = jnp.sum(grad_mixed.astype(jnp.float32), axis=0)
    grad_normed = contract_features(grad_mixed, w_qkv)
    unused, norm_back_one = jax.vjp(normalize, state, gains[0], shifts[0])
    grad_in_part, gain_one, shift_one = norm_back_one(grad_normed)
    grad_state = grad_middle + grad_in_part
    grad_gains = jnp.stack([gain_one, gain_two])
    grad_shifts = jnp.stack(
        [shift_one, shift_two, column_sums[:width], column_sums[2 * width :], out_bias, down_bias]
    )
    return (
        grad_state,
        (grad_qkv, grad_out, grad_up, grad_down, grad_gains, grad_shifts, grad_upbias),
    )


def local(tokens, cotangent, w_qkv, w_out, w_up, w_down, gains, shifts, up_bias):
    position = lax.axis_index("ctx") * tokens.shape[0]
    state = tokens.astype(jnp.float32)
    saved = []
    for layer in range(LAYERS):
        weights = (
            *sent_together((w_qkv[layer], w_out[layer], w_up[layer]), "dp", 0, 1),
            lax.all_gather(w_down[layer], "dp", axis=0, tiled=True),
            *sent_together((gains[layer], shifts[layer]), "dp", 1, 0),
            lax.all_gather(up_bias[layer], "dp", axis=0, tiled=True),
        )
        state, kept = layer_forward(state, weights, position)
        saved.append((kept, None))
    output = state.astype(jnp.bfloat16)
    grad_state = cotangent.astype(jnp.float32)
    collected = [None] * LAYERS
    for layer in reversed(range(LAYERS)):
        kept, weights = saved[layer]
        weights = (
            *sent_together((w_qkv[layer], w_out[layer], w_up[layer]), "dp", 0, 1),
            lax.all_gather(w_down[layer], "dp", axis=0, tiled=True),
            *sent_together((gains[layer], shifts[layer]), "dp", 1, 0),
            lax.all_gather(up_bias[layer], "dp", axis=0, tiled=True),
        )
        grad_state, grads = layer_backward(kept, weights, grad_state, position)
        shares = (
            *tuple(
                (
                    part.astype(jnp.float32)
                    for part in in_one_piece(
                        (
                            grads[0].astype(jnp.bfloat16),
                            grads[1].astype(jnp.bfloat16),
                            grads[2].astype(jnp.bfloat16),
                        ),
                        "dp",
                        0,
                        1,
                    )
                )
            ),
            lax.psum_scatter(
                grads[3].astype(jnp.bfloat16), "dp", scatter_dimension=0, tiled=True
            ).astype(jnp.float32),
            *tuple(
                (
                    part.astype(jnp.float32)
                    for part in in_one_piece(
                        (grads[4].astype(jnp.bfloat16), grads[5].astype(jnp.bfloat16)), "dp", 1, 0
                    )
                )
            ),
            lax.psum_scatter(
                grads[6].astype(jnp.bfloat16), "dp", scatter_dimension=0, tiled=True
            ).astype(jnp.float32),
        )
        shares = (
            lax.psum(shares[0].astype(jnp.bfloat16), "ctx").astype(jnp.float32),
            lax.psum(shares[1].astype(jnp.bfloat16), "ctx").astype(jnp.float32),
            lax.psum(shares[2].astype(jnp.bfloat16), "ctx").astype(jnp.float32),
            lax.psum(shares[3].astype(jnp.bfloat16), "ctx").astype(jnp.float32),
            lax.psum(shares[4].astype(jnp.bfloat16), "ctx").astype(jnp.float32),
            lax.psum(shares[5].astype(jnp.bfloat16), "ctx").astype(jnp.float32),
            lax.psum(shares[6].astype(jnp.bfloat16), "ctx").astype(jnp.float32),
        )
        collected[layer] = shares
    stacked = [
        jnp.stack([collected[layer][member] for layer in range(LAYERS)]) for member in range(7)
    ]
    return (
        output,
        grad_state,
        stacked[0],
        stacked[1],
        stacked[2],
        stacked[3],
        stacked[4],
        stacked[5],
        stacked[6],
    )


def solution(mesh):
    placed = (
        P(("dp", "ctx"), None),
        P(("dp", "ctx"), None),
        P(None, "dp", None),
        P(None, "dp", None),
        P(None, "dp", None),
        P(None, "dp", None),
        P(None, None, "dp"),
        P(None, None, "dp"),
        P(None, "dp"),
    )
    return jax.shard_map(
        local,
        mesh=mesh,
        in_specs=placed,
        out_specs=(
            P(("dp", "ctx"), None),
            P(("dp", "ctx"), None),
            P(None, "dp", None),
            P(None, "dp", None),
            P(None, "dp", None),
            P(None, "dp", None),
            P(None, None, "dp"),
            P(None, None, "dp"),
            P(None, "dp"),
        ),
        check_vma=False,
    )
```

profile of v0, /device:TPU:1, one launch (start us, length us, event | category | flops | bytes accessed | tf_op | source)
XLA Modules:
  0.0 1271.3 jit_solution(17953638390078792452)
XLA Ops:
  11.2 22.3 %all-gather.5 = bf16[8,96,8]{1,2,0:T(8,128)(2,1)S(1)} all-gather(bf16[1,96,8]{1,2,0:T(8,128)(2,1)S(1)} %maximum_bitcast_fusion.1), channel_id=1, replica_groups=mesh['dp'=8,'ctx'=16] {'dp'}, dimensions={0}, use_global_device_ids=true | all-gather | bytes 13824 | tf_op jit(solution)/shard_map/all_gather | solution.py:18
  33.6 21.6 %all-gather.4 = bf16[8,96,8]{1,2,0:T(8,128)(2,1)S(1)} all-gather(bf16[1,96,8]{1,2,0:T(8,128)(2,1)S(1)} %maximum_bitcast_fusion), channel_id=1, replica_groups=mesh['dp'=8,'ctx'=16] {'dp'}, dimensions={0}, use_global_device_ids=true | all-gather | bytes 13824 | tf_op jit(solution)/shard_map/all_gather | solution.py:18
  57.6 59.2 %all-gather.15.cloned.1.call-done = bf16[768,6144]{1,0:T(8,128)(2,1)} async-done(((bf16[96,6144]{1,0:T(8,128)(2,1)}), bf16[768,6144]{1,0:T(8,128)(2,1)}) %all-gather.15.cloned.1.call-update) | async-done | bytes 9437200 | tf_op jit(solution)/shard_map/all_gather | solution.py:18
  124.5 20.0 %all-gather = bf16[1,3072]{1,0:T(2,128)(2,1)S(1)} all-gather(bf16[1,384]{1,0:T(2,128)(2,1)S(1)} %get-tuple-element.642), channel_id=2, replica_groups=mesh['dp'=8,'ctx'=16] {'dp'}, dimensions={1}, use_global_device_ids=true | all-gather | bytes 6912 | tf_op jit(solution)/shard_map/all_gather | solution.py:271
  147.8 36.9 %all-gather.17.cloned.1.call-done = bf16[2048,1536]{1,0:T(8,128)(2,1)} async-done(((bf16[128,1536]{1,0:T(8,128)(2,1)}), bf16[2048,1536]{1,0:T(8,128)(2,1)}) %all-gather.17.cloned.1.call-update) | async-done | bytes 6291472 | tf_op jit(solution)/shard_map/all_gather | solution.py:18
  205.9 9.2 fusion.195
  221.0 21.1 %all-gather.27.cloned.1.call-done = bf16[1,3072,768]{2,1,0:T(8,128)(2,1)} async-done(((bf16[1,384,768]{2,1,0:T(8,128)(2,1)}), bf16[1,3072,768]{2,1,0:T(8,128)(2,1)}) %all-gather.27.cloned.1.call-update) | async-done | bytes 4718608 | tf_op jit(solution)/shard_map/all_gather | solution.py:269
  245.8 98.9 %all-gather.19.cloned.1.call-done = bf16[768,6144]{1,0:T(8,128)(2,1)} async-done(((bf16[96,6144]{1,0:T(8,128)(2,1)}), bf16[768,6144]{1,0:T(8,128)(2,1)}) %all-gather.19.cloned.1.call-update) | async-done | bytes 9437200 | tf_op jit(solution)/shard_map/all_gather | solution.py:18
  349.7 20.1 %all-gather.2 = bf16[1,3072]{1,0:T(2,128)(2,1)S(1)} all-gather(bf16[1,384]{1,0:T(2,128)(2,1)S(1)} %copy-done.108), channel_id=4, replica_groups=mesh['dp'=8,'ctx'=16] {'dp'}, dimensions={1}, use_global_device_ids=true | all-gather | bytes 6912 | tf_op jit(solution)/shard_map/all_gather | solution.py:271
  371.3 41.2 %all-gather.21.cloned.1.call-done = bf16[2048,1536]{1,0:T(8,128)(2,1)} async-done(((bf16[128,1536]{1,0:T(8,128)(2,1)}), bf16[2048,1536]{1,0:T(8,128)(2,1)}) %all-gather.21.cloned.1.call-update) | async-done | bytes 6291472 | tf_op jit(solution)/shard_map/all_gather | solution.py:18
  433.7 8.5 fusion.199
  447.6 22.7 %all-gather.29.cloned.1.call-done = bf16[1,3072,768]{2,1,0:T(8,128)(2,1)} async-done(((bf16[1,384,768]{2,1,0:T(8,128)(2,1)}), bf16[1,3072,768]{2,1,0:T(8,128)(2,1)}) %all-gather.29.cloned.1.call-update) | async-done | bytes 4718608 | tf_op jit(solution)/shard_map/all_gather | solution.py:269
  488.6 26.4 %all_gather.61 = f32[24,2048]{1,0:T(8,128)} all-gather(f32[24,128]{1,0:T(8,128)S(1)} %pad_maximum_fusion.10), channel_id=1, replica_groups=mesh['dp'=8,'ctx'=16] {'ctx'}, dimensions={1}, use_global_device_ids=true | all-gather | bytes 208896 | tf_op jit(solution)/shard_map/all_gather | solution.py:18
  515.8 7.8 while.48
  527.0 21.3 %all-gather.23.cloned.1.call-done = bf16[2048,1536]{1,0:T(8,128)(2,1)} async-done(((bf16[128,1536]{1,0:T(8,128)(2,1)}), bf16[2048,1536]{1,0:T(8,128)(2,1)}) %all-gather.23.cloned.1.call-update) | async-done | bytes 6291472 | tf_op jit(solution)/shard_map/all_gather | solution.py:18
  548.3 5.9 fusion.182
  555.0 67.5 %while.49 = (s32[]{:T(128)}, f32[128,12,64]{0,2,1:T(8,128)}, f32[128,12,64]{0,2,1:T(8,128)S(1)}, bf16[2048,768]{1,0:T(8,128)(2,1)}, bf16[128,12,64]{0,2,1:T(8,12...) while((s32[]{:T(128)}, f32[128,12,64]{0,2,1:T(8,128)}, ...), condition=%wide.region_18.19_spmd.clone, body=%wide.region_17.18_spmd.clone.sunk | while | flops 409207424 | bytes 21574908 | solution.py:161
  629.0 5.0 fusion.202
  634.1 5.0 multiply_reduce_fusion.2
  656.8 21.8 %all_gather.63 = f32[24,2048]{1,0:T(8,128)} all-gather(f32[24,128]{1,0:T(8,128)S(1)} %pad_maximum_fusion.11), channel_id=1, replica_groups=mesh['dp'=8,'ctx'=16] {'ctx'}, dimensions={1}, use_global_device_ids=true | all-gather | bytes 208896 | tf_op jit(solution)/shard_map/all_gather | solution.py:18
  679.4 7.9 while.50
  694.7 9.1 all-gather.25.cloned.1.call-done
  703.8 6.0 fusion.181
  710.7 67.6 %while.51 = (s32[]{:T(128)}, f32[128,12,64]{0,2,1:T(8,128)}, f32[128,12,64]{0,2,1:T(8,128)S(1)}, bf16[2048,768]{1,0:T(8,128)(2,1)}, bf16[128,12,64]{0,2,1:T(8,12...) while((s32[]{:T(128)}, f32[128,12,64]{0,2,1:T(8,128)}, ...), condition=%wide.region_27.28_spmd.clone, body=%wide.region_26.27_spmd.clone.sunk | while | flops 409207424 | bytes 21574908 | solution.py:161
  792.5 5.1 convolution_convert_fusion.1
  812.5 98.4 %reduce-scatter.11.cloned.1.call-done = bf16[96,6144]{1,0:T(8,128)(2,1)} async-done(((bf16[768,6144]{1,0:T(8,128)(2,1)}), bf16[96,6144]{1,0:T(8,128)(2,1)}) %reduce-scatter.11.cloned.1.call-update) | async-done | bytes 1179664 | tf_op jit(solution)/shard_map/reduce_scatter | solution.py:29
  916.2 54.0 %reduce-scatter.17.cloned.1.call-done = bf16[384,768]{1,0:T(8,128)(2,1)} async-done(((bf16[3072,768]{1,0:T(8,128)(2,1)}), bf16[384,768]{1,0:T(8,128)(2,1)}) %reduce-scatter.17.cloned.1.call-update) | async-done | bytes 589840 | tf_op jit(solution)/shard_map/reduce_scatter | solution.py:303
  970.2 59.2 %reduce-scatter.15.cloned.1.call-done = bf16[384,768]{1,0:T(8,128)(2,1)} async-done(((bf16[3072,768]{1,0:T(8,128)(2,1)}), bf16[384,768]{1,0:T(8,128)(2,1)}) %reduce-scatter.15.cloned.1.call-update) | async-done | bytes 589840 | tf_op jit(solution)/shard_map/reduce_scatter | solution.py:303
  1034.9 25.0 %all-reduce.4 = (bf16[3072]{0:T(1024)(128)(2,1)S(1)}, bf16[3072]{0:T(1024)(128)(2,1)S(1)}) all-reduce(bf16[3072]{0:T(1024)(128)(2,1)S(1)} %copy-done.105, bf16[3072]{0:T(1024)(128)(2,1)S(1)} %copy-done.106), channel_id=13, replica_groups=mesh['dp'=8,'ctx'=16] {'dp'}, use_global_device_ids=true, to_apply=%region_66.67.clone | all-reduce | flops 6144 | bytes 24576
  1065.7 35.7 %reduce-scatter.19.cloned.1.call-done = bf16[96,8]{1,0:T(8,128)(2,1)} async-done(((bf16[768,8]{1,0:T(8,128)(2,1)}), bf16[96,8]{1,0:T(8,128)(2,1)}) %reduce-scatter.19.cloned.1.call-update) | async-done | bytes 1552
  1103.1 39.0 %all-reduce.2 = (bf16[1,2,96]{2,1,0:T(2,128)(2,1)S(1)}, bf16[1,2,96]{2,1,0:T(2,128)(2,1)S(1)}, bf16[1,6,96]{2,1,0:T(8,128)(2,1)S(1)}, bf16[1,6,96]{2,1,0:T(8,128...) all-reduce(bf16[1,2,96]{2,1,0:T(2,128)(2,1)S(1)} %bitcast.387, ...), channel_id=1, replica_groups=mesh['dp'=8,'ctx'=16] {'ctx'}, use_global_device_ids=true, to_apply=%region_59.60 | all-reduce | flops 2304 | bytes 9216 | tf_op jit(solution)/shard_map/psum | solution.py:323
  1143.9 113.9 %all-reduce.7.cloned.1.call-done = (bf16[1,96,2304]{2,1,0:T(8,128)(2,1)}, bf16[1,96,2304]{2,1,0:T(8,128)(2,1)}, bf16[1,96,768]{2,1,0:T(8,128)(2,1)}, bf16[1,96,7...) async-done(((bf16[1,96,2304]{2,1,0:T(8,128)(2,1)}, ...) | async-done | bytes 3538960 | tf_op jit(solution)/shard_map/psum | solution.py:319
  (593 shorter events, 341.3 us)
Async XLA Ops:
  7.2 109.7 %all-gather.15.cloned.1.call-start = ((), (), s32[]{:S(2)}) async-start(), calls=%async_computation.6 | async-start | bytes 10616832 | tf_op jit(solution)/shard_map/all_gather | solution.py:18
  11.0 173.6 %all-gather.17.cloned.1.call-start = ((), (), s32[]{:S(2)}) async-start(), calls=%async_computation.7 | async-start | bytes 6684672 | tf_op jit(solution)/shard_map/all_gather | solution.py:18
  56.7 64.8 %copy-start.69 = (f32[768]{0:T(1024)}, f32[768]{0:T(1024)S(1)}, u32[]{:S(2)}) copy-start(f32[768]{0:T(1024)S(1)} %get-tuple-element.671) | copy-start | bytes 9220
  56.7 64.8 %copy-start.73 = (f32[768]{0:T(1024)}, f32[768]{0:T(1024)S(1)}, u32[]{:S(2)}) copy-start(f32[768]{0:T(1024)S(1)} %get-tuple-element.483) | copy-start | bytes 9220
  57.4 64.1 %copy-start.86 = (f32[128]{0:T(128)}, f32[128]{0:T(128)S(1)}, u32[]{:S(2)}) copy-start(f32[128]{0:T(128)S(1)} %broadcast_multiply_fusion.3) | copy-start | bytes 1540
  57.6 63.9 %copy-start.126 = (f32[128]{0:T(128)}, f32[128]{0:T(128)S(1)}, u32[]{:S(2)}) copy-start(f32[128]{0:T(128)S(1)} %fusion.150) | copy-start | bytes 1540
  57.6 63.8 %copy-start.93 = (f32[128]{0:T(128)}, f32[128]{0:T(128)S(1)}, u32[]{:S(2)}) copy-start(f32[128]{0:T(128)S(1)} %fusion.158) | copy-start | bytes 1540
  121.5 120.6 %all-gather.27.cloned.1.call-start = ((), (), s32[]{:S(2)}) async-start(), calls=%async_computation.16 | async-start | bytes 5308416 | tf_op jit(solution)/shard_map/all_gather | solution.py:269
  122.7 222.1 %all-gather.19.cloned.1.call-start = ((), (), s32[]{:S(2)}) async-start(), calls=%async_computation.8 | async-start | bytes 10616832 | tf_op jit(solution)/shard_map/all_gather | solution.py:18
  123.9 288.6 %all-gather.21.cloned.1.call-start = ((), (), s32[]{:S(2)}) async-start(), calls=%async_computation.9 | async-start | bytes 6684672 | tf_op jit(solution)/shard_map/all_gather | solution.py:18
  242.1 102.7 %copy-start.81 = (f32[2304]{0:T(1024)S(1)}, f32[2304]{0:T(1024)}, u32[]{:S(2)}) copy-start(f32[2304]{0:T(1024)} %get-tuple-element.637) | copy-start | bytes 27652
  245.6 196.7 %copy-start.5 = (f32[128,768]{1,0:T(8,128)}, f32[128,768]{1,0:T(8,128)S(1)}, u32[]{:S(2)}) copy-start(f32[128,768]{1,0:T(8,128)S(1)} %get-tuple-element.654) | copy-start | bytes 1179652
  245.6 103.5 %copy-start.88 = (f32[128]{0:T(128)}, f32[128]{0:T(128)S(1)}, u32[]{:S(2)}) copy-start(f32[128]{0:T(128)S(1)} %broadcast_multiply_fusion.1) | copy-start | bytes 1540
  245.8 103.3 %copy-start.130 = (f32[128]{0:T(128)}, f32[128]{0:T(128)S(1)}, u32[]{:S(2)}) copy-start(f32[128]{0:T(128)S(1)} %multiply_reduce_fusion.9) | copy-start | bytes 1540
  245.8 103.3 %copy-start.103 = (f32[128]{0:T(128)}, f32[128]{0:T(128)S(1)}, u32[]{:S(2)}) copy-start(f32[128]{0:T(128)S(1)} %fusion.160) | copy-start | bytes 1540
  349.1 121.2 %all-gather.29.cloned.1.call-start = ((), (), s32[]{:S(2)}) async-start(), calls=%async_computation.17 | async-start | bytes 5308416 | tf_op jit(solution)/shard_map/all_gather | solution.py:269
  349.7 198.6 %all-gather.23.cloned.1.call-start = ((), (), s32[]{:S(2)}) async-start(), calls=%async_computation.10 | async-start | bytes 6684672 | tf_op jit(solution)/shard_map/all_gather | solution.py:18
  484.7 219.1 %all-gather.25.cloned.1.call-start = ((), (), s32[]{:S(2)}) async-start(), calls=%async_computation.11 | async-start | bytes 6684672 | tf_op jit(solution)/shard_map/all_gather | solution.py:18
  642.8 164.3 %reduce-scatter.13.cloned.1.call-start = ((), (), s32[]{:S(2)}) async-start(), calls=%async_computation.13 | async-start | bytes 10616832 | tf_op jit(solution)/shard_map/reduce_scatter | solution.py:29
  650.3 260.5 %reduce-scatter.11.cloned.1.call-start = ((), (), s32[]{:S(2)}) async-start(), calls=%async_computation.12 | async-start | bytes 10616832 | tf_op jit(solution)/shard_map/reduce_scatter | solution.py:29
  710.7 68.7 %copy-start.70 = (f32[768]{0:T(1024)S(1)}, f32[768]{0:T(1024)}, u32[]{:S(2)}) copy-start(f32[768]{0:T(1024)} %copy-done.69) | copy-start | bytes 9220
  710.7 68.7 %copy-start.74 = (f32[768]{0:T(1024)S(1)}, f32[768]{0:T(1024)}, u32[]{:S(2)}) copy-start(f32[768]{0:T(1024)} %copy-done.73) | copy-start | bytes 9220
  710.7 68.7 %copy-start.87 = (f32[128]{0:T(128)S(1)}, f32[128]{0:T(128)}, u32[]{:S(2)}) copy-start(f32[128]{0:T(128)} %copy-done.86) | copy-start | bytes 1540
  710.7 68.7 %copy-start.94 = (f32[128]{0:T(128)S(1)}, f32[128]{0:T(128)}, u32[]{:S(2)}) copy-start(f32[128]{0:T(128)} %copy-done.93) | copy-start | bytes 1540
  786.5 183.8 %reduce-scatter.17.cloned.1.call-start = ((), (), s32[]{:S(2)}) async-start(), calls=%async_computation.15 | async-start | bytes 5308416 | tf_op jit(solution)/shard_map/reduce_scatter | solution.py:303
  791.6 237.8 %reduce-scatter.15.cloned.1.call-start = ((), (), s32[]{:S(2)}) async-start(), calls=%async_computation.14 | async-start | bytes 5308416 | tf_op jit(solution)/shard_map/reduce_scatter | solution.py:303
  797.8 265.2 %reduce-scatter.21.cloned.1.call-start = ((), (), s32[]{:S(2)}) async-start(), calls=%async_computation.19 | async-start | bytes 221184
  800.1 301.3 %reduce-scatter.19.cloned.1.call-start = ((), (), s32[]{:S(2)}) async-start(), calls=%async_computation.18 | async-start | bytes 221184
  805.3 452.4 %all-reduce.7.cloned.1.call-start = ((), (), s32[]{:S(2)}) async-start(), calls=%async_computation.20 | async-start | bytes 7077888 | tf_op jit(solution)/shard_map/psum | solution.py:319
  810.9 218.6 %copy-start.132 = (u32[128]{0:T(128)S(1)}, u32[128]{0:T(128)}, u32[]{:S(2)}) copy-start(u32[128]{0:T(128)} %constant.140) | copy-start | bytes 1540
  810.9 219.8 %copy-start.14 = (f32[128,768]{1,0:T(8,128)S(1)}, f32[128,768]{1,0:T(8,128)}, u32[]{:S(2)}) copy-start(f32[128,768]{1,0:T(8,128)} %copy-done.12) | copy-start | bytes 1179652
  810.9 219.8 %copy-start.113 = (f32[768]{0:T(1024)S(1)}, f32[768]{0:T(1024)}, u32[]{:S(2)}) copy-start(f32[768]{0:T(1024)} %get-tuple-element.473) | copy-start | bytes 9220
  (128 other events, 951.3 us)
Sparse Core Ops, SparseCore 0:
  11.2 105.6 all-gather.14
  121.6 62.9 all-gather.16
  186.3 55.7 all-gather.26
  244.2 100.5 all-gather.18
  349.2 63.2 all-gather.20
  414.6 55.7 all-gather.28
  484.8 63.4 all-gather.22
  642.9 60.8 all-gather.24
  706.2 100.8 reduce-scatter.12
  809.4 101.4 reduce-scatter.10
  913.3 56.8 reduce-scatter.16
  972.5 56.8 reduce-scatter.14
  1032.3 30.6 reduce-scatter.20
  1065.4 36.0 reduce-scatter.18
  1105.0 152.7 all-reduce.6
where the time goes:
time: 1280 us; the launch traced here: 1270 us
  waiting for transfers between devices  677 us (53%)
  blocking collectives  196 us (15%)
  matrix products  185 us (14%)
  local copies, waits for them, and re-layouts  149 us (12%)
  other arithmetic  45.1 us (4%)
  between operations  16.6 us (1%)
    all_gather x6, waiting for transfers between devices, sent_together(): filled = lax.all_gather(both, axis, axis=dim, tiled=True)  267 us
    psum x1, waiting for transfers between devices, local(): lax.psum(shares[0].astype(jnp.bfloat16), 'ctx').astype(jnp.float32)  114 us
    reduce_scatter x2, waiting for transfers between devices, local(): lax.psum_scatter(grads[3].astype(jnp.bfloat16), 'dp', scatter_dimension=0...  113 us
    reduce_scatter x2, waiting for transfers between devices, in_one_piece(): lax.psum_scatter(both, axis, scatter_dimension=dim, tiled=True)  100 us
    all_gather x4, blocking collectives, sent_together(): filled = lax.all_gather(both, axis, axis=dim, tiled=True)  92.2 us
    all_gather x2, waiting for transfers between devices, local(): lax.all_gather(w_down[layer], 'dp', axis=0, tiled=True)  43.8 us
    all_gather x2, blocking collectives, local(): lax.all_gather(up_bias[layer], 'dp', axis=0, tiled=True)  40.1 us
    split x10, local copies, waits for them, and re-layouts, sent_together(): jnp.split(filled, [sum(widths[:k]) for k in range(1, len(widths))], axis=...  39.6 us
  transfers between devices with their start and end apart: 15, of which 15 were waited for; matrix products, arithmetic and copies ran while one was open for 19% of the time, Pallas kernels for 0%

commit v1 on v0

v1 whole, which is shorter than its diff:
```python
import jax
import jax.numpy as jnp
from jax import lax
from jax.experimental import pallas as pl
from jax.experimental.pallas import tpu as pltpu
from jax.sharding import PartitionSpec as P

HEADS = 12
HEAD = 64
LAYERS = 2
D = 768
FF = 3072
DP = 8
BLK = 128
CHIPS = 8
CORES = 2
PAIR = CORES * BLK
OWN_HEADS = HEADS // CORES
SEQ = CHIPS * PAIR
FF_PART = FF // DP // CORES
FF_HALF = FF // CORES
QKV_HALF = 3 * D // CORES
PIECE = 640
EPSILON = 1e-05
NEGATIVE = -1e30
SAME_CORE = [[CORES * u + k for u in range(CHIPS)] for k in range(CORES)]
OTHER_CORE = [(i, i ^ 1) for i in range(CHIPS * CORES)]
BF = jnp.bfloat16
F32 = jnp.float32


def dot(left, right, ldim, rdim):
    return lax.dot_general(
        left, right, (((ldim,), (rdim,)), ((), ())), preferred_element_type=F32
    )


def swap(value):
    return lax.ppermute(value, "ctx", OTHER_CORE)


def diagonal_mask(size):
    key = lax.broadcasted_iota(jnp.int32, (size, size), 0)
    query = lax.broadcasted_iota(jnp.int32, (size, size), 1)
    return key <= query


def attend_kernel(qkv_ref, out_ref, ctx_ref, lse_ref):
    step = PAIR
    keys = [qkv_ref[j, HEAD : 2 * HEAD, :] for j in range(CHIPS)]
    allowed = diagonal_mask(step)
    for i in range(CHIPS):
        query = qkv_ref[i, 0:HEAD, :]
        scores = [dot(keys[j], query, 0, 0) for j in range(i + 1)]
        scores[i] = jnp.where(allowed, scores[i], NEGATIVE)
        peak = scores[0].max(axis=0, keepdims=True)
        for j in range(1, i + 1):
            peak = jnp.maximum(peak, scores[j].max(axis=0, keepdims=True))
        total = jnp.zeros((1, step), F32)
        accum = jnp.zeros((HEAD, step), F32)
        for j in range(i + 1):
            weights = jnp.exp(scores[j] - peak)
            total = total + weights.sum(axis=0, keepdims=True)
            accum = accum + dot(qkv_ref[j, 2 * HEAD : 3 * HEAD, :], weights.astype(BF), 1, 0)
        context = accum / total
        out_ref[2 * i] = context[:, :BLK].astype(BF)
        out_ref[2 * i + 1] = context[:, BLK:].astype(BF)
        ctx_ref[i] = context
        lse_ref[i] = peak + jnp.log(total)


def attend(qkv):
    return pl.pallas_call(
        attend_kernel,
        out_shape=(
            jax.ShapeDtypeStruct((CORES * CHIPS, HEAD, BLK), BF),
            jax.ShapeDtypeStruct((CHIPS, HEAD, PAIR), F32),
            jax.ShapeDtypeStruct((CHIPS, 1, PAIR), F32),
        ),
        compiler_params=pltpu.CompilerParams(vmem_limit_bytes=40 * 1024 * 1024),
        name="attend",
    )(qkv)


def attend_back_kernel(qkv_ref, grad_ref, ctx_ref, lse_ref, out_ref, dq_ref):
    allowed = diagonal_mask(PAIR)
    grads, deltas = [], []
    for i in range(CHIPS):
        grad = jnp.concatenate([grad_ref[2 * i], grad_ref[2 * i + 1]], axis=1)
        grads.append(grad)
        deltas.append((grad.astype(F32) * ctx_ref[i]).sum(axis=0, keepdims=True))
    for j in range(CHIPS):
        key = qkv_ref[j, HEAD : 2 * HEAD, :]
        value = qkv_ref[j, 2 * HEAD : 3 * HEAD, :]
        grad_key = jnp.zeros((HEAD, PAIR), F32)
        grad_value = jnp.zeros((HEAD, PAIR), F32)
        for i in range(j, CHIPS):
            query = qkv_ref[i, 0:HEAD, :]
            probs = jnp.exp(dot(key, query, 0, 0) - lse_ref[i])
            if i == j:
                probs = jnp.where(allowed, probs, 0.0)
            grad_probs = dot(value, grads[i], 0, 0)
            grad_scores = (probs * (grad_probs - deltas[i])).astype(BF)
            grad_value = grad_value + dot(grads[i], probs.astype(BF), 1, 1)
            grad_key = grad_key + dot(query, grad_scores, 1, 1)
            grad_query = dot(key, grad_scores, 1, 0)
            if j == 0:
                dq_ref[i] = grad_query
            else:
                dq_ref[i] = dq_ref[i] + grad_query
        out_ref[j, 0:HEAD, :] = (dq_ref[j] * HEAD**-0.5).astype(BF)
        out_ref[j, HEAD : 2 * HEAD, :] = grad_key.astype(BF)
        out_ref[j, 2 * HEAD : 3 * HEAD, :] = grad_value.astype(BF)


def attend_back(qkv, grad, context, logsum):
    return pl.pallas_call(
        attend_back_kernel,
        out_shape=jax.ShapeDtypeStruct((CHIPS, 3 * HEAD, PAIR), BF),
        scratch_shapes=[pltpu.VMEM((CHIPS, HEAD, PAIR), F32)],
        compiler_params=pltpu.CompilerParams(vmem_limit_bytes=40 * 1024 * 1024),
        name="attend_back",
    )(qkv, grad, context, logsum)


def norm_parts(values):
    average = jnp.mean(values, axis=-1, keepdims=True)
    centered = values - average
    spread = jnp.mean(centered * centered, axis=-1, keepdims=True)
    scale = lax.rsqrt(spread + EPSILON)
    return centered * scale, scale


def norm_back(grad, hat, scale, gain):
    scaled = grad * gain
    first = jnp.mean(scaled, axis=-1, keepdims=True)
    second = jnp.mean(scaled * hat, axis=-1, keepdims=True)
    part = scale * (scaled - first - hat * second)
    return part, jnp.sum(grad * hat, axis=0), jnp.sum(grad, axis=0)


def ordered(mine, other, core):
    three = jnp.concatenate([mine, other, mine], axis=0)
    return lax.dynamic_slice_in_dim(three, core * BLK, PAIR, 0)


def across_chips(value):
    return lax.all_to_all(value, "ctx", 0, 0, axis_index_groups=SAME_CORE, tiled=True)


def layer_forward(state, weights, core):
    w_qkv, w_out, w_up, w_down, gains, shifts, qkv_bias, up_bias = weights
    hat_one, scale_one = norm_parts(state)
    mine = (hat_one * gains[0] + shifts[0]).astype(BF)
    normed = ordered(mine, swap(mine), core)
    mixed = (dot(w_qkv, normed, 0, 1) + qkv_bias[:, None]).reshape(OWN_HEADS, 3, HEAD, PAIR)
    factor = jnp.array([HEAD**-0.5, 1.0, 1.0], F32).reshape(1, 3, 1, 1)
    qkv = (mixed * factor).astype(BF).reshape(OWN_HEADS, 3 * HEAD, PAIR)
    qkv = jnp.concatenate([qkv, jnp.zeros((CHIPS - OWN_HEADS, 3 * HEAD, PAIR), BF)], axis=0)
    qkv = across_chips(qkv)
    out, context, logsum = attend(qkv)
    out = lax.all_to_all(out, "ctx", 0, 0, tiled=True)
    attended = out[:HEADS].reshape(D, BLK)
    middle = state + (dot(attended, w_out, 0, 0) + shifts[4])
    hat_two, scale_two = norm_parts(middle)
    mine_two = (hat_two * gains[1] + shifts[1]).astype(BF)
    normed_two = jnp.concatenate([mine_two, swap(mine_two)], axis=0)
    upper = dot(normed_two, w_up, 1, 0) + up_bias
    active = jax.nn.gelu(upper).astype(BF)
    partial = dot(active, w_down, 1, 0)
    result = middle + (partial[:BLK] + swap(partial[BLK:].astype(BF)).astype(F32) + shifts[5])
    kept = (
        hat_one, scale_one, normed, qkv, context, logsum,
        attended, hat_two, scale_two, normed_two, upper, active,
    )
    return result, kept


def half_to_full(vector, parts, core):
    piece = vector.reshape(parts, 1, -1)
    slot = lax.broadcasted_iota(jnp.int32, (parts, CORES, piece.shape[2]), 1)
    return jnp.where(slot == core, piece, 0.0).reshape(-1)


def layer_backward(kept, weights, grad_result, core):
    (
        hat_one, scale_one, normed, qkv, context, logsum,
        attended, hat_two, scale_two, normed_two, upper, active,
    ) = kept
    w_qkv, w_out, w_up, w_down, gains, shifts, qkv_bias, up_bias = weights
    mine = grad_result.astype(BF)
    down_bias = jnp.sum(mine.astype(F32), axis=0)
    both = jnp.concatenate([mine, swap(mine)], axis=0)
    grad_active = dot(both, w_down, 1, 1)
    gelu_back = jax.vjp(jax.nn.gelu, upper)[1]
    grad_upper = gelu_back(grad_active)[0].astype(BF)
    partial = dot(grad_upper, w_up, 1, 1)
    grad_normed_two = partial[:BLK] + swap(partial[BLK:].astype(BF)).astype(F32)
    grad_down = dot(active, both, 0, 0).astype(BF)
    grad_up = dot(normed_two, grad_upper, 0, 0).astype(BF)
    grad_upbias = jnp.sum(grad_upper.astype(F32), axis=0)
    shares_up = lax.psum_scatter(grad_up, "dp", scatter_dimension=0, tiled=True)
    shares_down = lax.psum_scatter(grad_down, "dp", scatter_dimension=0, tiled=True)
    part, gain_two, shift_two = norm_back(grad_normed_two, hat_two, scale_two, gains[1])
    grad_middle = grad_result + part
    branch = grad_middle.astype(BF)
    out_bias = jnp.sum(branch.astype(F32), axis=0)
    grad_out_t = dot(w_out, branch, 1, 1).astype(BF).reshape(HEADS, HEAD, BLK)
    grad_out_t = jnp.concatenate(
        [grad_out_t, jnp.zeros((CHIPS * CORES - HEADS, HEAD, BLK), BF)], axis=0
    )
    grad_context = lax.all_to_all(grad_out_t, "ctx", 0, 0, tiled=True)
    grad_out = dot(attended, branch, 1, 0)
    grad_mixed = across_chips(attend_back(qkv, grad_context, context, logsum))
    grad_mixed = grad_mixed[:OWN_HEADS].reshape(QKV_HALF, PAIR)
    partial = dot(grad_mixed, w_qkv, 0, 1)
    mine = lax.dynamic_slice_in_dim(partial, core * BLK, BLK, 0)
    other = lax.dynamic_slice_in_dim(partial, (1 - core) * BLK, BLK, 0)
    grad_normed = mine + swap(other.astype(BF)).astype(F32)
    grad_qkv = dot(normed, grad_mixed, 0, 1).astype(BF)
    sums = jnp.sum(grad_mixed.astype(F32), axis=1).reshape(OWN_HEADS, 3, HEAD)
    part, gain_one, shift_one = norm_back(grad_normed, hat_one, scale_one, gains[0])
    grad_state = grad_middle + part
    columns = D // CORES
    keep = lax.dynamic_slice_in_dim(grad_out, core * columns, columns, 1)
    give = lax.dynamic_slice_in_dim(grad_out, (1 - core) * columns, columns, 1)
    grad_out = (keep + swap(give.astype(BF)).astype(F32)).astype(BF)
    upbias = half_to_full(grad_upbias, DP, core).reshape(DP, 4, D // DP)
    upbias = upbias.transpose(1, 0, 2).reshape(4, D)
    small = jnp.stack(
        [
            gain_one, gain_two, shift_one, shift_two,
            half_to_full(sums[:, 0], OWN_HEADS, core), half_to_full(sums[:, 2], OWN_HEADS, core),
            out_bias, down_bias, upbias[0], upbias[1], upbias[2], upbias[3],
        ]
    )
    small = small + swap(small)
    small = jnp.pad(small.astype(BF).T, ((0, 0), (0, 8 * PIECE - 3 * FF_HALF - 12)))
    shares = lax.psum_scatter(
        jnp.concatenate([grad_qkv, grad_out, small], axis=1), "dp", scatter_dimension=0, tiled=True
    )
    rows = D // DP
    flat = jnp.concatenate([shares_up, shares_down[:rows], shares_down[rows:], shares], axis=1)
    pieces = flat.reshape(rows, CHIPS, PIECE).transpose(1, 0, 2)
    summed = jnp.sum(across_chips(pieces).astype(F32), axis=0).astype(BF)
    return grad_state, lax.all_gather(summed, "ctx", axis=0, tiled=False)


def unpack(whole):
    rows = D // DP
    halves = whole.reshape(CHIPS, CORES, rows, PIECE).transpose(1, 2, 0, 3)
    halves = halves.reshape(CORES, rows, CHIPS * PIECE).astype(F32)
    up, down_a, down_b, qkv, out, small = jnp.split(
        halves, [FF_HALF, FF_HALF + D, 2 * FF_HALF, 2 * FF_HALF + QKV_HALF, 3 * FF_HALF], axis=2
    )
    up = up.reshape(CORES, rows, DP, FF_PART).transpose(1, 2, 0, 3).reshape(rows, FF)
    down = jnp.stack([down_a, down_b], axis=1).reshape(FF // DP, D)
    qkv = qkv.reshape(CORES, rows, OWN_HEADS, 3, HEAD).transpose(1, 3, 2, 0, 4)
    qkv = qkv.reshape(rows, 3 * D)
    out = out.transpose(1, 0, 2).reshape(rows, D)
    small = small[0, :, :12].T
    return qkv, out, up, down, small[0:2], small[2:8], small[8:12].reshape(FF // DP)


def local(tokens, cotangent, w_qkv, w_out, w_up, w_down, gains, shifts, up_bias):
    core = lax.rem(lax.axis_index("ctx"), CORES)
    rows = D // DP

    def pick(value, axis):
        return lax.dynamic_index_in_dim(value, core, axis, keepdims=False)

    def gather(value, axis=0):
        return lax.all_gather(value, "dp", axis=axis, tiled=True)

    vectors = jnp.concatenate(
        [gains.reshape(-1, rows), shifts.reshape(-1, rows), up_bias.reshape(-1, rows)], axis=0
    )
    vectors = lax.all_gather(vectors, "dp", axis=0, tiled=False).transpose(1, 0, 2).astype(F32)
    all_gains = vectors[:4].reshape(LAYERS, 2, D)
    all_shifts = vectors[4:16].reshape(LAYERS, 6, D)
    all_up = vectors[16:24].reshape(LAYERS, CORES, 2, DP, FF_PART // 2).transpose(0, 1, 3, 2, 4)
    weights = []
    for layer in range(LAYERS):
        qkv_part = pick(w_qkv[layer].reshape(rows, 3, OWN_HEADS, CORES, HEAD), 3)
        qkv_part = qkv_part.transpose(0, 2, 1, 3).reshape(rows, QKV_HALF)
        first = gather(jnp.concatenate([qkv_part, w_out[layer]], axis=1))
        up = gather(pick(w_up[layer].reshape(rows, DP, CORES, FF_PART), 2).reshape(rows, FF_HALF))
        down = gather(pick(w_down[layer].reshape(CORES, FF_PART, D), 0))
        shift = all_shifts[layer]
        zeros = jnp.zeros((OWN_HEADS, HEAD), F32)
        qkv_bias = jnp.stack(
            [
                pick(shift[2].reshape(OWN_HEADS, CORES, HEAD), 1),
                zeros,
                pick(shift[3].reshape(OWN_HEADS, CORES, HEAD), 1),
            ],
            axis=1,
        ).reshape(QKV_HALF)
        bias = pick(all_up[layer], 0).reshape(FF_HALF)
        weights.append(
            (
                first[:, :QKV_HALF], first[:, QKV_HALF:], up, down,
                all_gains[layer], shift, qkv_bias, bias,
            )
        )
    state = tokens.astype(F32)
    saved = []
    for layer in range(LAYERS):
        state, kept = layer_forward(state, weights[layer], core)
        saved.append(kept)
    output = state.astype(BF)
    grad = cotangent.astype(F32)
    collected = [None] * LAYERS
    for layer in reversed(range(LAYERS)):
        grad, whole = layer_backward(saved[layer], weights[layer], grad, core)
        collected[layer] = unpack(whole)
    stacked = [jnp.stack([collected[layer][m] for layer in range(LAYERS)]) for m in range(7)]
    return (output, grad, *stacked)


def solution(mesh):
    placed = (
        P(("dp", "ctx"), None),
        P(("dp", "ctx"), None),
        P(None, "dp", None),
        P(None, "dp", None),
        P(None, "dp", None),
        P(None, "dp", None),
        P(None, None, "dp"),
        P(None, None, "dp"),
        P(None, "dp"),
    )
    return jax.shard_map(
        local,
        mesh=mesh,
        in_specs=placed,
        out_specs=placed,
        check_vma=False,
    )
```

time: 1280 us -> 746 us (0.58)
  waiting for transfers between devices: 677 us -> 347 us
  matrix products: 185 us -> 54.2 us
  blocking collectives: 196 us -> 115 us
  local copies, waits for them, and re-layouts: 149 us -> 81.7 us
  starting transfers between devices: 1.28 us -> 50.5 us
  Pallas kernels: 0 us -> 31 us
    all_gather x8, waiting for transfers between devices: 310 us -> 172 us  [the longest x6 106 us: gather(): return lax.all_gather(value, 'dp', axis=axis, tiled=True)]
    dot_general x56 -> x24, matrix products: 185 us -> 54.2 us  [dot(): lax.dot_general(left, right, (((ldim,), (rdim,)), ((), ())), preferred_el...]
    psum x1 -> x0, waiting for transfers between devices: 114 us -> none  [local(): lax.psum(shares[0].astype(jnp.bfloat16), 'ctx').astype(jnp.float32)]
    all_gather x6 -> x1, blocking collectives: 132 us -> 25.9 us  [local(): lax.all_gather(vectors, 'dp', axis=0, tiled=False).transpose(1, 0, 2)]
    reduce_scatter x4 -> x6, waiting for transfers between devices: 213 us -> 123 us  [the longest x2 51.6 us: layer_backward(): lax.psum_scatter(jnp.concatenate([grad_qkv, grad_out, small], axis=1), 'd...]
    all_to_all x0 -> x5, blocking collectives: none -> 89.1 us  [the longest x4 73.8 us: across_chips(): lax.all_to_all(value, 'ctx', 0, 0, axis_index_groups=SAME_CORE, tiled=True)]
    dynamic_slice x34 -> x10, local copies, waits for them, and re-layouts: 62.5 us -> 6.54 us  [pick(): return lax.dynamic_index_in_dim(value, core, axis, keepdims=False)]
    all_to_all x0 -> x5, waiting for transfers between devices: none -> 50 us  [the longest x2 27.5 us: across_chips(): lax.all_to_all(value, 'ctx', 0, 0, axis_index_groups=SAME_CORE, tiled=True)]
  transfers between devices with their start and end apart: 15 -> 35, of which waited for: 15 -> 18; matrix products, arithmetic and copies ran while one was open for 19% -> 20% of each run, Pallas kernels for 0% -> 4%
where the time goes in v1:
time: 746 us; the launch traced here: 739 us
  waiting for transfers between devices  347 us (47%)
  blocking collectives  115 us (15%)
  local copies, waits for them, and re-layouts  81.7 us (11%)
  matrix products  54.2 us (7%)
  starting transfers between devices  50.5 us (7%)
  other arithmetic  43.2 us (6%)
  Pallas kernels  31 us (4%)
  between operations  15.8 us (2%)
    all_gather x6, waiting for transfers between devices, gather(): return lax.all_gather(value, 'dp', axis=axis, tiled=True)  106 us
    all_to_all x4, blocking collectives, across_chips(): lax.all_to_all(value, 'ctx', 0, 0, axis_index_groups=SAME_CORE, tiled=True)  73.8 us
    all_gather x2, waiting for transfers between devices, layer_backward(): return (grad_state, lax.all_gather(summed, 'ctx', axis=0, tiled=False))  66.5 us
    dot_general x24, matrix products, dot(): lax.dot_general(left, right, (((ldim,), (rdim,)), ((), ())), preferred_el...  54.2 us
    reduce_scatter x2, waiting for transfers between devices, layer_backward(): lax.psum_scatter(jnp.concatenate([grad_qkv, grad_out, small], axis=1), 'd...  51.6 us
    reduce_scatter x2, waiting for transfers between devices, layer_backward(): shares_up = lax.psum_scatter(grad_up, 'dp', scatter_dimension=0, tiled=True)  42.2 us
    reduce_scatter x2, waiting for transfers between devices, layer_backward(): lax.psum_scatter(grad_down, 'dp', scatter_dimension=0, tiled=True)  29 us
    all_to_all x2, waiting for transfers between devices, across_chips(): lax.all_to_all(value, 'ctx', 0, 0, axis_index_groups=SAME_CORE, tiled=True)  27.5 us
  transfers between devices with their start and end apart: 35, of which 18 were waited for; matrix products, arithmetic and copies ran while one was open for 20% of the time, Pallas kernels for 4%

profile of v1, /device:TPU:1, one launch (start us, length us, event | category | flops | bytes accessed | tf_op | source)
XLA Modules:
  0.0 738.5 jit_solution(16079097689694987675)
XLA Ops:
  20.1 25.9 %all-gather = bf16[192,96]{1,0:T(8,128)(2,1)S(1)} all-gather(bf16[24,96]{1,0:T(8,128)(2,1)S(1)} %pad_maximum_fusion.21), channel_id=2, replica_groups=mesh['dp'=8,'ctx'=16] {'dp'}, dimensions={0}, use_global_device_ids=true | all-gather | bytes 41472 | tf_op jit(solution)/shard_map/all_gather | solution.py:278
  46.9 5.6 collective-permute-start
  60.9 20.7 %all_to_all.50.qkv_ref = bf16[8,192,256]{2,1,0:T(8,128)(2,1)S(1)} all-to-all(bf16[8,192,256]{2,1,0:T(8,128)(2,1)S(1)} %concatenate.54), channel_id=1, replica_groups={{0,2,4,6,8,10,12,14},{1,3,5,7,9,11,13,15},{16,18,20,22,24,26,28,30},{17..., dimensions={0} | all-to-all | bytes 1572864 | tf_op jit(solution)/shard_map/all_to_all | solution.py:148
  81.6 5.4 attend.2
  87.0 4.9 all-to-all-start.1
  92.2 8.4 %all-to-all-done.1 = bf16[16,64,128]{2,1,0:T(8,128)(2,1)S(1)} async-done(((bf16[16,64,128]{2,1,0:T(8,128)(2,1)}), bf16[16,64,128]{2,1,0:T(8,128)(2,1)S(1)}, u32[]{:S(2)}, u32[]{:S(2)}) %all-to-all-start.1) | async-done | bytes 262176 | tf_op jit(solution)/shard_map/all_to_all | solution.py:162
  110.2 39.8 %all-gather.22.cloned.1.call-done = bf16[1,1536,768]{2,1,0:T(8,128)(2,1)} async-done(((bf16[1,192,768]{2,1,0:T(8,128)(2,1)}), bf16[1,1536,768]{2,1,0:T(8,128)(2,1)}) %all-gather.22.cloned.1.call-update) | async-done | bytes 2359312 | tf_op jit(solution)/shard_map/all_gather | solution.py:273
  154.0 5.3 collective-permute-start.2
  164.0 31.9 %all-gather.18.cloned.1.call-done = bf16[768,1920]{1,0:T(8,128)(2,1)} async-done(((bf16[96,1920]{1,0:T(8,128)(2,1)}), bf16[768,1920]{1,0:T(8,128)(2,1)}) %all-gather.18.cloned.1.call-update) | async-done | bytes 2949136 | tf_op jit(solution)/shard_map/all_gather | solution.py:273
  198.4 16.7 %all_to_all.51.qkv_ref = bf16[8,192,256]{2,1,0:T(8,128)(2,1)S(1)} all-to-all(bf16[8,192,256]{2,1,0:T(8,128)(2,1)S(1)} %concatenate.58), channel_id=1, replica_groups={{0,2,4,6,8,10,12,14},{1,3,5,7,9,11,13,15},{16,18,20,22,24,26,28,30},{17..., dimensions={0} | all-to-all | bytes 1572864 | tf_op jit(solution)/shard_map/all_to_all | solution.py:148
  215.1 5.5 attend.3
  220.5 10.1 %all-to-all-start.3 = ((bf16[16,64,128]{2,1,0:T(8,128)(2,1)}), bf16[16,64,128]{2,1,0:T(8,128)(2,1)}, u32[]{:S(2)}, u32[]{:S(2)}) async-start(bf16[16,64,128]{2,1,0:T(8,128)(2,1)} %get-tuple-element.16), calls=%async_computation.3 | async-start | bytes 524288 | tf_op jit(solution)/shard_map/all_to_all | solution.py:162
  231.4 8.1 %all-to-all-done.3 = bf16[16,64,128]{2,1,0:T(8,128)(2,1)} async-done(((bf16[16,64,128]{2,1,0:T(8,128)(2,1)}), bf16[16,64,128]{2,1,0:T(8,128)(2,1)}, u32[]{:S(2)}, u32[]{:S(2)}) %all-to-all-start.3) | async-done | bytes 262176 | tf_op jit(solution)/shard_map/all_to_all | solution.py:162
  254.4 31.8 %all-gather.24.cloned.1.call-done = bf16[1,1536,768]{2,1,0:T(8,128)(2,1)} async-done(((bf16[1,192,768]{2,1,0:T(8,128)(2,1)}), bf16[1,1536,768]{2,1,0:T(8,128)(2,1)}) %all-gather.24.cloned.1.call-update) | async-done | bytes 2359312 | tf_op jit(solution)/shard_map/all_gather | solution.py:273
  286.3 3.9 convert_reduce_fusion
  291.1 5.3 collective-permute-start.7
  303.0 15.3 %all_to_all.52.grad_ref = bf16[16,64,128]{2,1,0:T(8,128)(2,1)S(1)} all-to-all(bf16[16,64,128]{2,1,0:T(8,128)(2,1)S(1)} %concatenate.61), channel_id=1, replica_groups=mesh['dp'=8,'ctx'=16] {'ctx'}, dimensions={0} | all-to-all | bytes 524288 | tf_op jit(solution)/shard_map/all_to_all | solution.py:212
  318.3 10.1 %attend_back.2 = bf16[8,192,256]{2,1,0:T(8,128)(2,1)} custom-call(bf16[8,192,256]{2,1,0:T(8,128)(2,1)S(1)} %all_to_all.51.qkv_ref, bf16[16,64,128]{2,1,0:T(8,128)(2,1)S(1)} %all_to_all.52.grad_ref, f32[8,64,256]{2,1,0:T(8,128)S(1)} %get-tuple-element.17.ctx_ref, f32[8,1,256]{2,1,0:T(1,128)S(1)} %get-tuple-element.18.lse_ref), custom_call_target="tpu_custom_call" | custom-call | tf_op jit(solution)/shard_map/attend_back/pallas_call | solution.py:117
  332.0 14.4 %all-to-all-done.5 = bf16[8,192,256]{2,1,0:T(8,128)(2,1)S(1)} async-done(((bf16[8,192,256]{2,1,0:T(8,128)(2,1)}), bf16[8,192,256]{2,1,0:T(8,128)(2,1)S(1)}, u32[]{:S(2)}, u32[]{:S(2)}) %all-to-all-start.5) | async-done | bytes 786464 | tf_op jit(solution)/shard_map/all_to_all | solution.py:148
  360.4 4.4 convert_reduce_fusion.1
  374.5 3.7 all-to-all-start.6
  381.0 6.0 all-to-all-done.6.grad_ref
  387.0 10.1 %attend_back.3 = bf16[8,192,256]{2,1,0:T(8,128)(2,1)} custom-call(bf16[8,192,256]{2,1,0:T(8,128)(2,1)S(1)} %all_to_all.50.qkv_ref, bf16[16,64,128]{2,1,0:T(8,128)(2,1)S(1)} %all-to-all-done.6.grad_ref, f32[8,64,256]{2,1,0:T(8,128)S(1)} %get-tuple-element.19.ctx_ref, f32[8,1,256]{2,1,0:T(1,128)S(1)} %get-tuple-element.20.lse_ref), custom_call_target="tpu_custom_call" | custom-call | tf_op jit(solution)/shard_map/attend_back/pallas_call | solution.py:117
  397.1 3.7 all-to-all-start.7
  402.2 13.1 %all-to-all-done.7 = bf16[8,192,256]{2,1,0:T(8,128)(2,1)S(1)} async-done(((bf16[8,192,256]{2,1,0:T(8,128)(2,1)}), bf16[8,192,256]{2,1,0:T(8,128)(2,1)S(1)}, u32[]{:S(2)}, u32[]{:S(2)}) %all-to-all-start.7) | async-done | bytes 786464 | tf_op jit(solution)/shard_map/all_to_all | solution.py:148
  465.1 18.2 %all_to_all.53 = bf16[8,96,640]{2,1,0:T(8,128)(2,1)S(1)} all-to-all(bf16[8,96,640]{2,1,0:T(8,128)(2,1)S(1)} %bitcast.181), channel_id=1, replica_groups={{0,2,4,6,8,10,12,14},{1,3,5,7,9,11,13,15},{16,18,20,22,24,26,28,30},{17..., dimensions={0} | all-to-all | bytes 1966080 | tf_op jit(solution)/shard_map/all_to_all | solution.py:148
  484.1 29.0 %reduce-scatter.9.cloned.1.call-done = bf16[192,768]{1,0:T(8,128)(2,1)} async-done(((bf16[1536,768]{1,0:T(8,128)(2,1)}), bf16[192,768]{1,0:T(8,128)(2,1)}) %reduce-scatter.9.cloned.1.call-update) | async-done | bytes 294928 | tf_op jit(solution)/shard_map/reduce_scatter | solution.py:203
  514.2 42.1 %reduce-scatter.7.cloned.1.call-done = bf16[96,1536]{1,0:T(8,128)(2,1)} async-done(((bf16[768,1536]{1,0:T(8,128)(2,1)}), bf16[96,1536]{1,0:T(8,128)(2,1)}) %reduce-scatter.7.cloned.1.call-update) | async-done | bytes 294928 | tf_op jit(solution)/shard_map/reduce_scatter | solution.py:202
  556.3 48.7 %reduce-scatter.11.cloned.1.call-done = bf16[96,2048]{1,0:T(8,128)(2,1)} async-done(((bf16[768,2048]{1,0:T(8,128)(2,1)}), bf16[96,2048]{1,0:T(8,128)(2,1)}) %reduce-scatter.11.cloned.1.call-update) | async-done | bytes 393232 | tf_op jit(solution)/shard_map/reduce_scatter | solution.py:239
  606.3 18.2 %all_to_all.54 = bf16[8,96,640]{2,1,0:T(8,128)(2,1)S(1)} all-to-all(bf16[8,96,640]{2,1,0:T(8,128)(2,1)S(1)} %bitcast.182), channel_id=1, replica_groups={{0,2,4,6,8,10,12,14},{1,3,5,7,9,11,13,15},{16,18,20,22,24,26,28,30},{17..., dimensions={0} | all-to-all | bytes 1966080 | tf_op jit(solution)/shard_map/all_to_all | solution.py:148
  626.3 33.5 %all-gather.28.cloned.1.call-done = bf16[1536,640]{1,0:T(8,128)(2,1)} async-done(((bf16[96,640]{1,0:T(8,128)(2,1)}), bf16[1536,640]{1,0:T(8,128)(2,1)}) %all-gather.28.cloned.1.call-update) | async-done | bytes 1966096 | tf_op jit(solution)/shard_map/all_gather | solution.py:246
  676.0 33.0 %all-gather.26.cloned.1.call-done = bf16[1536,640]{1,0:T(8,128)(2,1)} async-done(((bf16[96,640]{1,0:T(8,128)(2,1)}), bf16[1536,640]{1,0:T(8,128)(2,1)}) %all-gather.26.cloned.1.call-update) | async-done | bytes 1966096 | tf_op jit(solution)/shard_map/all_gather | solution.py:246
  (499 shorter events, 190.2 us)
Async XLA Ops:
  7.2 51.2 %all-gather.14.cloned.1.call-start = ((), (), s32[]{:S(2)}) async-start(), calls=%async_computation.16 | async-start | bytes 3317760 | tf_op jit(solution)/shard_map/all_gather | solution.py:273
  10.2 96.3 %all-gather.16.cloned.1.call-start = ((), (), s32[]{:S(2)}) async-start(), calls=%async_computation.17 | async-start | bytes 2654208 | tf_op jit(solution)/shard_map/all_gather | solution.py:273
  16.1 133.9 %all-gather.22.cloned.1.call-start = ((), (), s32[]{:S(2)}) async-start(), calls=%async_computation.26 | async-start | bytes 2654208 | tf_op jit(solution)/shard_map/all_gather | solution.py:273
  18.2 177.7 %all-gather.18.cloned.1.call-start = ((), (), s32[]{:S(2)}) async-start(), calls=%async_computation.18 | async-start | bytes 3317760 | tf_op jit(solution)/shard_map/all_gather | solution.py:273
  19.9 227.1 %all-gather.20.cloned.1.call-start = ((), (), s32[]{:S(2)}) async-start(), calls=%async_computation.19 | async-start | bytes 2654208 | tf_op jit(solution)/shard_map/all_gather | solution.py:273
  46.9 10.9 %collective-permute-start = (bf16[128,768]{1,0:T(8,128)(2,1)S(1)}, bf16[128,768]{1,0:T(8,128)(2,1)S(1)}, u32[]{:S(2)}, u32[]{:S(2)}) collective-permute-start(bf16[128,768]{1,0:T(8,128)(2,1)S(1)} %fusion.49), channel_id=1, source_target_pairs={{0,1},{1,0},{2,3},{3,2},{4,5},{5,4},{6,7},{7,6},{8,9},{9,8},{10,11... | collective-permute-start | bytes 589832 | tf_op jit(solution)/shard_map/ppermute | solution.py:39
  87.0 13.6 %all-to-all-start.1 = ((bf16[16,64,128]{2,1,0:T(8,128)(2,1)}), bf16[16,64,128]{2,1,0:T(8,128)(2,1)S(1)}, u32[]{:S(2)}, u32[]{:S(2)}) async-start(bf16[16,64,128]{2,1,0:T(8,128)(2,1)} %get-tuple-element.15), calls=%async_computation.1 | async-start | bytes 524288 | tf_op jit(solution)/shard_map/all_to_all | solution.py:162
  91.9 194.4 %all-gather.24.cloned.1.call-start = ((), (), s32[]{:S(2)}) async-start(), calls=%async_computation.27 | async-start | bytes 2654208 | tf_op jit(solution)/shard_map/all_gather | solution.py:273
  102.8 3.7 collective-permute-start.1
  154.0 6.4 collective-permute-start.2
  220.5 18.9 %all-to-all-start.3 = ((bf16[16,64,128]{2,1,0:T(8,128)(2,1)}), bf16[16,64,128]{2,1,0:T(8,128)(2,1)}, u32[]{:S(2)}, u32[]{:S(2)}) async-start(bf16[16,64,128]{2,1,0:T(8,128)(2,1)} %get-tuple-element.16), calls=%async_computation.3 | async-start | bytes 524288 | tf_op jit(solution)/shard_map/all_to_all | solution.py:162
  230.6 229.3 %reduce-scatter.15.cloned.1.call-start = ((), (), s32[]{:S(2)}) async-start(), calls=%async_computation.24 | async-start | bytes 2654208 | tf_op jit(solution)/shard_map/reduce_scatter | solution.py:203
  230.7 14.7 %collective-permute-start.6 = (bf16[128,768]{1,0:T(8,128)(2,1)}, bf16[128,768]{1,0:T(8,128)(2,1)}, u32[]{:S(2)}, u32[]{:S(2)}) collective-permute-start(bf16[128,768]{1,0:T(8,128)(2,1)} %param.12), channel_id=1, source_target_pairs={{0,1},{1,0},{2,3},{3,2},{4,5},{5,4},{6,7},{7,6},{8,9},{9,8},{10,11... | collective-permute-start | bytes 589832 | tf_op jit(solution)/shard_map/ppermute | solution.py:39
  243.8 3.1 collective-permute-start.4
  291.1 7.9 %collective-permute-start.7 = (bf16[128,768]{1,0:T(8,128)(2,1)S(1)}, bf16[128,768]{1,0:T(8,128)(2,1)S(1)}, u32[]{:S(2)}, u32[]{:S(2)}) collective-permute-start(bf16[128,768]{1,0:T(8,128)(2,1)S(1)} %slice.502), channel_id=1, source_target_pairs={{0,1},{1,0},{2,3},{3,2},{4,5},{5,4},{6,7},{7,6},{8,9},{9,8},{10,11... | collective-permute-start | bytes 589832 | tf_op jit(solution)/shard_map/ppermute | solution.py:39
  297.5 2.5 collective-permute-start.5
  328.4 18.0 %all-to-all-start.5 = ((bf16[8,192,256]{2,1,0:T(8,128)(2,1)}), bf16[8,192,256]{2,1,0:T(8,128)(2,1)S(1)}, u32[]{:S(2)}, u32[]{:S(2)}) async-start(bf16[8,192,256]{2,1,0:T(8,128)(2,1)} %attend_back.2), calls=%async_computation.5 | async-start | bytes 1572864 | tf_op jit(solution)/shard_map/all_to_all | solution.py:148
  332.0 129.0 %reduce-scatter.13.cloned.1.call-start = ((), (), s32[]{:S(2)}) async-start(), calls=%async_computation.23 | async-start | bytes 2654208 | tf_op jit(solution)/shard_map/reduce_scatter | solution.py:202
  357.0 3.4 collective-permute-start.9
  365.7 4.7 collective-permute-start.10
  367.6 10.7 %collective-permute-start.14 = (bf16[768,384]{1,0:T(8,128)(2,1)}, bf16[768,384]{1,0:T(8,128)(2,1)}, u32[]{:S(2)}, u32[]{:S(2)}) collective-permute-start(bf16[768,384]{1,0:T(8,128)(2,1)} %dynamic-slice_convert_fusion), channel_id=1, source_target_pairs={{0,1},{1,0},{2,3},{3,2},{4,5},{5,4},{6,7},{7,6},{8,9},{9,8},{10,11... | collective-permute-start | bytes 1769480 | tf_op jit(solution)/shard_map/ppermute | solution.py:39
  374.5 12.5 %all-to-all-start.6 = ((bf16[16,64,128]{2,1,0:T(8,128)(2,1)}), bf16[16,64,128]{2,1,0:T(8,128)(2,1)S(1)}, u32[]{:S(2)}, u32[]{:S(2)}) async-start(bf16[16,64,128]{2,1,0:T(8,128)(2,1)} %concatenate.63), calls=%async_computation.6 | async-start | bytes 524288 | tf_op jit(solution)/shard_map/all_to_all | solution.py:212
  397.1 18.2 %all-to-all-start.7 = ((bf16[8,192,256]{2,1,0:T(8,128)(2,1)}), bf16[8,192,256]{2,1,0:T(8,128)(2,1)S(1)}, u32[]{:S(2)}, u32[]{:S(2)}) async-start(bf16[8,192,256]{2,1,0:T(8,128)(2,1)} %attend_back.3), calls=%async_computation.7 | async-start | bytes 1572864 | tf_op jit(solution)/shard_map/all_to_all | solution.py:148
  400.8 63.0 %reduce-scatter.17.cloned.1.call-start = ((), (), s32[]{:S(2)}) async-start(), calls=%async_computation.25 | async-start | bytes 3538944 | tf_op jit(solution)/shard_map/reduce_scatter | solution.py:239
  417.9 2.7 collective-permute-start.15
  426.4 86.8 %reduce-scatter.9.cloned.1.call-start = ((), (), s32[]{:S(2)}) async-start(), calls=%async_computation.21 | async-start | bytes 2654208 | tf_op jit(solution)/shard_map/reduce_scatter | solution.py:203
  430.6 125.7 %reduce-scatter.7.cloned.1.call-start = ((), (), s32[]{:S(2)}) async-start(), calls=%async_computation.20 | async-start | bytes 2654208 | tf_op jit(solution)/shard_map/reduce_scatter | solution.py:202
  434.1 170.9 %reduce-scatter.11.cloned.1.call-start = ((), (), s32[]{:S(2)}) async-start(), calls=%async_computation.22 | async-start | bytes 3538944 | tf_op jit(solution)/shard_map/reduce_scatter | solution.py:239
  436.4 12.5 %collective-permute-start.12 = (bf16[768,384]{1,0:T(8,128)(2,1)}, bf16[768,384]{1,0:T(8,128)(2,1)}, u32[]{:S(2)}, u32[]{:S(2)}) collective-permute-start(bf16[768,384]{1,0:T(8,128)(2,1)} %dynamic-slice_convert_fusion.1), channel_id=1, source_target_pairs={{0,1},{1,0},{2,3},{3,2},{4,5},{5,4},{6,7},{7,6},{8,9},{9,8},{10,11... | collective-permute-start | bytes 1769480 | tf_op jit(solution)/shard_map/ppermute | solution.py:39
  448.3 2.8 collective-permute-start.11
  459.8 200.0 %all-gather.28.cloned.1.call-start = ((), (), s32[]{:S(2)}) async-start(), calls=%async_computation.29 | async-start | bytes 2088960 | tf_op jit(solution)/shard_map/all_gather | solution.py:246
  484.1 224.9 %all-gather.26.cloned.1.call-start = ((), (), s32[]{:S(2)}) async-start(), calls=%async_computation.28 | async-start | bytes 2088960 | tf_op jit(solution)/shard_map/all_gather | solution.py:246
  (93 other events, 819.9 us)
Sparse Core Ops, SparseCore 0:
  10.3 43.7 all-gather.13
  56.3 50.1 all-gather.15
  108.7 41.1 all-gather.21
  152.0 43.8 all-gather.17
  198.0 46.7 all-gather.19
  246.3 39.9 all-gather.23
  289.3 45.3 reduce-scatter.14
  360.5 36.9 reduce-scatter.12
  426.5 37.3 reduce-scatter.16
  466.7 46.4 reduce-scatter.8
  515.6 40.6 reduce-scatter.6
  558.6 46.4 reduce-scatter.10
  608.0 51.7 all-gather.27
  662.1 46.8 all-gather.25

commit v2 on v1

--- a/solution.py
+++ b/solution.py
@@ -20,7 +20,6 @@
 FF_PART = FF // DP // CORES
 FF_HALF = FF // CORES
 QKV_HALF = 3 * D // CORES
-PIECE = 640
 EPSILON = 1e-05
 NEGATIVE = -1e30
 SAME_CORE = [[CORES * u + k for u in range(CHIPS)] for k in range(CORES)]
@@ -33,6 +32,103 @@
     return lax.dot_general(
         left, right, (((ldim,), (rdim,)), ((), ())), preferred_element_type=F32
     )
+
+
+def ring(axis, step, scale):
+    size = 4
+    count = 2 * size * scale
+    moves = []
+    for i in range(count):
+        block, low = i // scale, i % scale
+        pair, at = block // size, block % size
+        moves.append((i, (pair * size + (at + step) % size) * scale + low))
+    return lambda value: lax.ppermute(value, axis, moves)
+
+
+def across(axis, scale):
+    count = 8 * scale
+    return lambda value: lax.ppermute(
+        value, axis, [(i, (i + count // 2) % count) for i in range(count)]
+    )
+
+
+def places(axis, scale):
+    block = lax.axis_index(axis) // scale
+    pair, at = block // 4, block % 4
+    return [[((pair + far) % 2) * 4 + (at + step) % 4 for step in range(4)] for far in range(2)]
+
+
+def gather_start(value, axis, scale):
+    value = value[None]
+    far = across(axis, scale)(value)
+    own_up, own_down = ring(axis, 1, scale)(value), ring(axis, -1, scale)(value)
+    return value, far, own_up, own_down
+
+
+def gather_go_on(begun, axis, scale, after_one=None, after_two=None):
+    if after_one is not None:
+        begun = tie(begun, after_one)[0]
+    value, far, own_up, own_down = begun
+    up, down = ring(axis, 1, scale), ring(axis, -1, scale)
+    far_up, far_down = up(far), down(far)
+    own_two = up(own_up)
+    if after_two is not None:
+        far_down = tie(far_down, after_two)[0]
+    far_two = down(far_down)
+    return value, own_up, own_two, own_down, far, far_up, far_two, far_down
+
+
+def join_kernel(where_ref, *refs):
+    pieces, parts = refs[:8], refs[8:]
+    for k in range(8):
+        at = 0
+        for part in parts:
+            rows = part.shape[1]
+            part[where_ref[k]] = pieces[k][0, at : at + rows]
+            at += rows
+
+
+def gather_end(pieces, axis, scale, *heights):
+    where = places(axis, scale)
+    where = jnp.stack([where[k // 4][-(k % 4) % 4] for k in range(8)]).astype(jnp.int32)
+    _, rows, width = pieces[0].shape
+    return pl.pallas_call(
+        join_kernel,
+        in_specs=[pl.BlockSpec(memory_space=pltpu.SMEM)]
+        + [pl.BlockSpec(memory_space=pltpu.VMEM)] * 8,
+        out_shape=[
+            jax.ShapeDtypeStruct((8, height, width), pieces[0].dtype) for height in heights or (rows,)
+        ],
+        compiler_params=pltpu.CompilerParams(vmem_limit_bytes=40 * 1024 * 1024),
+        name="join",
+    )(where, *pieces)
+
+
+def ring_scatter(value, axis, scale, after):
+    up, down, pair = ring(axis, 1, scale), ring(axis, -1, scale), across(axis, scale)
+    where = places(axis, scale)
+    value = value.reshape(8, value.shape[0] // 8, *value.shape[1:])
+
+    def part(far, step):
+        return lax.dynamic_index_in_dim(value, where[far][step], 0, keepdims=False)
+
+    def add(*terms):
+        total = terms[0].astype(F32)
+        for term in terms[1:]:
+            total = total + term.astype(F32)
+        return total.astype(BF)
+
+    own_two, far_two = up(part(0, 2)), down(part(1, 2))
+    far_up, own_down = up(part(1, 1)), down(part(0, 3))
+    own_two, far_two, far_up, own_down, after = tie(own_two, far_two, far_up, own_down, after)
+    own_up = up(add(part(0, 1), own_two))
+    far_down = down(add(part(1, 3), far_two))
+    far = pair(add(part(1, 0), far_up, far_down))
+    return add(part(0, 0), own_up, own_down, far), after
+
+
+def tie(*values):
+    return lax.optimization_barrier(values)
 
 
 def swap(value):
@@ -148,18 +244,22 @@
     return lax.all_to_all(value, "ctx", 0, 0, axis_index_groups=SAME_CORE, tiled=True)
 
 
-def layer_forward(state, weights, core):
-    w_qkv, w_out, w_up, w_down, gains, shifts, qkv_bias, up_bias = weights
+def layer_forward(state, w_qkv, rest_part, vectors, core):
+    gains, shifts, qkv_bias, up_bias = vectors
     hat_one, scale_one = norm_parts(state)
     mine = (hat_one * gains[0] + shifts[0]).astype(BF)
     normed = ordered(mine, swap(mine), core)
+    rest = gather_start(rest_part, "dp", 1)
     mixed = (dot(w_qkv, normed, 0, 1) + qkv_bias[:, None]).reshape(OWN_HEADS, 3, HEAD, PAIR)
     factor = jnp.array([HEAD**-0.5, 1.0, 1.0], F32).reshape(1, 3, 1, 1)
     qkv = (mixed * factor).astype(BF).reshape(OWN_HEADS, 3 * HEAD, PAIR)
     qkv = jnp.concatenate([qkv, jnp.zeros((CHIPS - OWN_HEADS, 3 * HEAD, PAIR), BF)], axis=0)
     qkv = across_chips(qkv)
     out, context, logsum = attend(qkv)
+    rest = gather_go_on(rest, "dp", 1, qkv, out)
     out = lax.all_to_all(out, "ctx", 0, 0, tiled=True)
+    rest = gather_end(rest, "dp", 1)[0].reshape(D, -1)
+    w_out, w_up, w_down = rest[:, :D], rest[:, D : D + FF_HALF], rest[:, D + FF_HALF : D + 2 * FF_HALF]
     attended = out[:HEADS].reshape(D, BLK)
     middle = state + (dot(attended, w_out, 0, 0) + shifts[4])
     hat_two, scale_two = norm_parts(middle)
@@ -167,13 +267,14 @@
     normed_two = jnp.concatenate([mine_two, swap(mine_two)], axis=0)
     upper = dot(normed_two, w_up, 1, 0) + up_bias
     active = jax.nn.gelu(upper).astype(BF)
-    partial = dot(active, w_down, 1, 0)
+    partial = dot(active[:, :D], w_down[:, :D], 1, 0) + dot(active[:, D:], w_down[:, D:], 1, 0)
     result = middle + (partial[:BLK] + swap(partial[BLK:].astype(BF)).astype(F32) + shifts[5])
     kept = (
         hat_one, scale_one, normed, qkv, context, logsum,
         attended, hat_two, scale_two, normed_two, upper, active,
     )
-    return result, kept
+    weights = (w_qkv, w_out, w_up, w_down, gains)
+    return result, kept, weights, rest
 
 
 def half_to_full(vector, parts, core):
@@ -182,16 +283,18 @@
     return jnp.where(slot == core, piece, 0.0).reshape(-1)
 
 
-def layer_backward(kept, weights, grad_result, core):
+def layer_backward(kept, weights, grad_result, core, earlier):
     (
         hat_one, scale_one, normed, qkv, context, logsum,
         attended, hat_two, scale_two, normed_two, upper, active,
     ) = kept
-    w_qkv, w_out, w_up, w_down, gains, shifts, qkv_bias, up_bias = weights
+    w_qkv, w_out, w_up, w_down, gains = weights
     mine = grad_result.astype(BF)
     down_bias = jnp.sum(mine.astype(F32), axis=0)
     both = jnp.concatenate([mine, swap(mine)], axis=0)
-    grad_active = dot(both, w_down, 1, 1)
+    grad_active = jnp.concatenate(
+        [dot(both, w_down[:, :D], 1, 1), dot(both, w_down[:, D:], 1, 1)], axis=1
+    )
     gelu_back = jax.vjp(jax.nn.gelu, upper)[1]
     grad_upper = gelu_back(grad_active)[0].astype(BF)
     partial = dot(grad_upper, w_up, 1, 1)
@@ -199,8 +302,6 @@
     grad_down = dot(active, both, 0, 0).astype(BF)
     grad_up = dot(normed_two, grad_upper, 0, 0).astype(BF)
     grad_upbias = jnp.sum(grad_upper.astype(F32), axis=0)
-    shares_up = lax.psum_scatter(grad_up, "dp", scatter_dimension=0, tiled=True)
-    shares_down = lax.psum_scatter(grad_down, "dp", scatter_dimension=0, tiled=True)
     part, gain_two, shift_two = norm_back(grad_normed_two, hat_two, scale_two, gains[1])
     grad_middle = grad_result + part
     branch = grad_middle.astype(BF)
@@ -211,7 +312,20 @@
     )
     grad_context = lax.all_to_all(grad_out_t, "ctx", 0, 0, tiled=True)
     grad_out = dot(attended, branch, 1, 0)
-    grad_mixed = across_chips(attend_back(qkv, grad_context, context, logsum))
+    columns = D // CORES
+    keep = lax.dynamic_slice_in_dim(grad_out, core * columns, columns, 1)
+    give = lax.dynamic_slice_in_dim(grad_out, (1 - core) * columns, columns, 1)
+    grad_out = (keep + swap(give.astype(BF)).astype(F32)).astype(BF)
+    wide = jnp.concatenate([grad_up, grad_down[:D], grad_down[D:], grad_out], axis=1)
+    grad_context, wide = tie(grad_context, wide)
+    shares = lax.psum_scatter(wide, "dp", scatter_dimension=0, tiled=True)
+    if earlier is not None:
+        grad_context, earlier = tie(grad_context, earlier)
+        earlier = chip_sum(earlier, 4096)
+    grad_mixed = attend_back(qkv, grad_context, context, logsum)
+    if earlier is not None:
+        grad_mixed, earlier = tie(grad_mixed, earlier)
+    grad_mixed = across_chips(grad_mixed)
     grad_mixed = grad_mixed[:OWN_HEADS].reshape(QKV_HALF, PAIR)
     partial = dot(grad_mixed, w_qkv, 0, 1)
     mine = lax.dynamic_slice_in_dim(partial, core * BLK, BLK, 0)
@@ -221,12 +335,11 @@
     sums = jnp.sum(grad_mixed.astype(F32), axis=1).reshape(OWN_HEADS, 3, HEAD)
     part, gain_one, shift_one = norm_back(grad_normed, hat_one, scale_one, gains[0])
     grad_state = grad_middle + part
-    columns = D // CORES
-    keep = lax.dynamic_slice_in_dim(grad_out, core * columns, columns, 1)
-    give = lax.dynamic_slice_in_dim(grad_out, (1 - core) * columns, columns, 1)
-    grad_out = (keep + swap(give.astype(BF)).astype(F32)).astype(BF)
-    upbias = half_to_full(grad_upbias, DP, core).reshape(DP, 4, D // DP)
-    upbias = upbias.transpose(1, 0, 2).reshape(4, D)
+    upbias = grad_upbias.reshape(2, D)
+    empty = jnp.zeros_like(upbias)
+    upbias = jnp.concatenate(
+        [jnp.where(core == 0, upbias, empty), jnp.where(core == 1, upbias, empty)], axis=0
+    )
     small = jnp.stack(
         [
             gain_one, gain_two, shift_one, shift_two,
@@ -235,31 +348,85 @@
         ]
     )
     small = small + swap(small)
-    small = jnp.pad(small.astype(BF).T, ((0, 0), (0, 8 * PIECE - 3 * FF_HALF - 12)))
-    shares = lax.psum_scatter(
-        jnp.concatenate([grad_qkv, grad_out, small], axis=1), "dp", scatter_dimension=0, tiled=True
-    )
+    small = jnp.pad(small.astype(BF).T, ((0, 0), (0, 128 - 12)))
+    grad_rest = jnp.concatenate([grad_qkv, small], axis=1)
+    if earlier is None:
+        grad_state, grad_rest = tie(grad_state, grad_rest)
+    return grad_state, shares, grad_rest, earlier
+
+
+def chip_sum(shares, width):
     rows = D // DP
-    flat = jnp.concatenate([shares_up, shares_down[:rows], shares_down[rows:], shares], axis=1)
-    pieces = flat.reshape(rows, CHIPS, PIECE).transpose(1, 0, 2)
-    summed = jnp.sum(across_chips(pieces).astype(F32), axis=0).astype(BF)
-    return grad_state, lax.all_gather(summed, "ctx", axis=0, tiled=False)
-
-
-def unpack(whole):
+    shares = jnp.pad(shares, ((0, 0), (0, width - shares.shape[1])))
+    pieces = shares.reshape(rows, CHIPS, width // CHIPS).transpose(1, 0, 2)
+    moved = lax.all_to_all(pieces, "ctx", 0, 0, axis_index_groups=SAME_CORE, tiled=True)
+    return jnp.sum(moved.astype(F32), axis=0).astype(BF)
+
+
+def to_all_chips(summed):
+    mine = gather_go_on(gather_start(summed, "ctx", CORES), "ctx", CORES)
+    mine = gather_end(mine, "ctx", CORES)[0]
+    return mine, swap(mine)
+
+
+def unpack_kernel(core_ref, *refs):
+    pairs, (qkv_ref, out_ref, up_ref, down_ref, small_ref, flat) = refs[:4], refs[4:]
     rows = D // DP
-    halves = whole.reshape(CHIPS, CORES, rows, PIECE).transpose(1, 2, 0, 3)
-    halves = halves.reshape(CORES, rows, CHIPS * PIECE).astype(F32)
-    up, down_a, down_b, qkv, out, small = jnp.split(
-        halves, [FF_HALF, FF_HALF + D, 2 * FF_HALF, 2 * FF_HALF + QKV_HALF, 3 * FF_HALF], axis=2
-    )
-    up = up.reshape(CORES, rows, DP, FF_PART).transpose(1, 2, 0, 3).reshape(rows, FF)
-    down = jnp.stack([down_a, down_b], axis=1).reshape(FF // DP, D)
-    qkv = qkv.reshape(CORES, rows, OWN_HEADS, 3, HEAD).transpose(1, 3, 2, 0, 4)
-    qkv = qkv.reshape(rows, 3 * D)
-    out = out.transpose(1, 0, 2).reshape(rows, D)
-    small = small[0, :, :12].T
-    return qkv, out, up, down, small[0:2], small[2:8], small[8:12].reshape(FF // DP)
+
+    @pl.when(pl.program_id(0) == 0)
+    def _():
+        first = core_ref[0] == 0
+        at = 0
+        for mine_ref, other_ref in (pairs[:2], pairs[2:]):
+            size = mine_ref.shape[2]
+            for c in range(CHIPS):
+                mine, other = mine_ref[c].astype(F32), other_ref[c].astype(F32)
+                flat[0, :, at : at + size] = jnp.where(first, mine, other)
+                flat[1, :, at : at + size] = jnp.where(first, other, mine)
+                at += size
+
+    def layer(mlp, rest):
+        def part(k, start, size):
+            low, high = start // 128 * 128, -(-(start + size) // 128) * 128
+            return flat[k, :, low:high][:, start - low : start - low + size]
+
+        for d in range(DP):
+            pieces = [
+                part(k, mlp + e * D + d * rows, rows) for k in range(CORES) for e in range(2)
+            ]
+            up_ref[0, :, d * 4 * rows : (d + 1) * 4 * rows] = jnp.concatenate(pieces, axis=1)
+        for k in range(CORES):
+            for e in range(2):
+                at = mlp + FF_HALF + e * D
+                down_ref[0, (2 * k + e) * rows : (2 * k + e + 1) * rows, :] = flat[k, :, at : at + D]
+            at = mlp + 2 * FF_HALF
+            out_ref[0, :, k * D // 2 : (k + 1) * D // 2] = flat[k, :, at : at + D // 2]
+        for t in range(3):
+            for u in range(OWN_HEADS):
+                pieces = [part(k, rest + (u * 3 + t) * HEAD, HEAD) for k in range(CORES)]
+                to = t * D + u * 2 * HEAD
+                qkv_ref[0, :, to : to + 2 * HEAD] = jnp.concatenate(pieces, axis=1)
+        small_ref[0] = flat[0, :, rest + QKV_HALF : rest + QKV_HALF + 128].T[:16]
+
+    late = 4096 + 2 * FF_HALF + D // 2
+    pl.when(pl.program_id(0) == 0)(lambda: layer(4096, late + QKV_HALF + 128))
+    pl.when(pl.program_id(0) == 1)(lambda: layer(0, late))
+
+
+def unpack(core, *pairs):
+    rows = D // DP
+    shapes = [(rows, 3 * D), (rows, D), (rows, FF), (FF // DP, D), (16, rows)]
+    return pl.pallas_call(
+        unpack_kernel,
+        grid=(LAYERS,),
+        in_specs=[pl.BlockSpec(memory_space=pltpu.SMEM)]
+        + [pl.BlockSpec(pair.shape, lambda i: (0, 0, 0)) for pair in pairs],
+        out_specs=[pl.BlockSpec((1, *shape), lambda i: (i, 0, 0)) for shape in shapes],
+        out_shape=[jax.ShapeDtypeStruct((LAYERS, *shape), F32) for shape in shapes],
+        scratch_shapes=[pltpu.VMEM((CORES, rows, 4096 + 6144), F32)],
+        compiler_params=pltpu.CompilerParams(vmem_limit_bytes=48 * 1024 * 1024),
+        name="unpack",
+    )(core.reshape(1), *pairs)
 
 
 def local(tokens, cotangent, w_qkv, w_out, w_up, w_down, gains, shifts, up_bias):
@@ -269,23 +436,31 @@
     def pick(value, axis):
         return lax.dynamic_index_in_dim(value, core, axis, keepdims=False)
 
-    def gather(value, axis=0):
-        return lax.all_gather(value, "dp", axis=axis, tiled=True)
-
     vectors = jnp.concatenate(
         [gains.reshape(-1, rows), shifts.reshape(-1, rows), up_bias.reshape(-1, rows)], axis=0
     )
-    vectors = lax.all_gather(vectors, "dp", axis=0, tiled=False).transpose(1, 0, 2).astype(F32)
+    vectors = jnp.pad(vectors.reshape(2, QKV_HALF), ((0, 14), (0, 0)))
+    weights = []
+    qkv_parts, rest_parts = [], []
+    for layer in range(LAYERS):
+        qkv_part = pick(w_qkv[layer].reshape(rows, 3, OWN_HEADS, CORES, HEAD), 3)
+        qkv_parts.append(qkv_part.transpose(0, 2, 1, 3).reshape(rows, QKV_HALF))
+        up = pick(w_up[layer].reshape(rows, DP, CORES, 2, rows), 2)
+        up = up.transpose(0, 2, 1, 3).reshape(rows, FF_HALF)
+        down = pick(w_down[layer].reshape(CORES, 2, rows, D), 0)
+        rest_parts.append([w_out[layer], up, down[0], down[1]])
+    first = gather_start(jnp.concatenate([qkv_parts[0], vectors], axis=0), "dp", 1)
+    first, vectors = gather_end(gather_go_on(first, "dp", 1), "dp", 1, rows, 16)
+    vectors = vectors[:, :2].reshape(DP, 24, rows).transpose(1, 0, 2).astype(F32)
     all_gains = vectors[:4].reshape(LAYERS, 2, D)
     all_shifts = vectors[4:16].reshape(LAYERS, 6, D)
-    all_up = vectors[16:24].reshape(LAYERS, CORES, 2, DP, FF_PART // 2).transpose(0, 1, 3, 2, 4)
-    weights = []
+    all_up = vectors[16:24].reshape(LAYERS, CORES, 2, DP, rows)
+    w_now = first.reshape(D, QKV_HALF)
+    rest_part = jnp.concatenate([*rest_parts[0], qkv_parts[1]], axis=1)
+    rest_part = tie(rest_part, w_now)[0]
+    state = tokens.astype(F32)
+    saved = []
     for layer in range(LAYERS):
-        qkv_part = pick(w_qkv[layer].reshape(rows, 3, OWN_HEADS, CORES, HEAD), 3)
-        qkv_part = qkv_part.transpose(0, 2, 1, 3).reshape(rows, QKV_HALF)
-        first = gather(jnp.concatenate([qkv_part, w_out[layer]], axis=1))
-        up = gather(pick(w_up[layer].reshape(rows, DP, CORES, FF_PART), 2).reshape(rows, FF_HALF))
-        down = gather(pick(w_down[layer].reshape(CORES, FF_PART, D), 0))
         shift = all_shifts[layer]
         zeros = jnp.zeros((OWN_HEADS, HEAD), F32)
         qkv_bias = jnp.stack(
@@ -297,25 +472,27 @@
             axis=1,
         ).reshape(QKV_HALF)
         bias = pick(all_up[layer], 0).reshape(FF_HALF)
-        weights.append(
-            (
-                first[:, :QKV_HALF], first[:, QKV_HALF:], up, down,
-                all_gains[layer], shift, qkv_bias, bias,
-            )
-        )
-    state = tokens.astype(F32)
-    saved = []
-    for layer in range(LAYERS):
-        state, kept = layer_forward(state, weights[layer], core)
-        saved.append(kept)
+        few = (all_gains[layer], shift, qkv_bias, bias)
+        state, kept, weights, rest = layer_forward(state, w_now, rest_part, few, core)
+        if layer + 1 < LAYERS:
+            w_now = rest[:, D + 2 * FF_HALF :]
+            rest_part = jnp.concatenate(rest_parts[1], axis=1)
+            rest_part = tie(rest_part, rest)[0]
+        saved.append((kept, weights))
     output = state.astype(BF)
     grad = cotangent.astype(F32)
-    collected = [None] * LAYERS
-    for layer in reversed(range(LAYERS)):
-        grad, whole = layer_backward(saved[layer], weights[layer], grad, core)
-        collected[layer] = unpack(whole)
-    stacked = [jnp.stack([collected[layer][m] for layer in range(LAYERS)]) for m in range(7)]
-    return (output, grad, *stacked)
+    grad, shares_one, rest_one, _ = layer_backward(*saved[1], grad, core, None)
+    grad, shares_two, rest_two, early = layer_backward(*saved[0], grad, core, shares_one)
+    rest = jnp.concatenate([rest_one, rest_two], axis=1)
+    rest, early = ring_scatter(rest, "dp", 1, early)
+    early = to_all_chips(early)
+    late = jnp.concatenate([shares_two, rest], axis=1)
+    late = to_all_chips(chip_sum(late, 6144))
+    grad_qkv, grad_out, grad_up, grad_down, small = unpack(core, *early, *late)
+    return (
+        output, grad, grad_qkv, grad_out, grad_up, grad_down,
+        small[:, 0:2], small[:, 2:8], small[:, 8:12].reshape(LAYERS, FF // DP),
+    )
 
 
 def solution(mesh):

time: 746 us -> 548 us (0.73)
  waiting for transfers between devices: 347 us -> 182 us
  blocking collectives: 115 us -> 43.2 us
  starting transfers between devices: 50.5 us -> 108 us
  local copies, waits for them, and re-layouts: 81.7 us -> 64.3 us
  matrix products: 54.2 us -> 39.3 us
  Pallas kernels: 31 us -> 45.8 us
    all_gather x8 -> x0, waiting for transfers between devices: 172 us -> none  [the longest x6 106 us: gather(): return lax.all_gather(value, 'dp', axis=axis, tiled=True)]
    ppermute x0 -> x42, waiting for transfers between devices: none -> 127 us  [the longest x36 97.5 us: ring(): return lambda value: lax.ppermute(value, axis, moves)]
    reduce_scatter x6 -> x2, waiting for transfers between devices: 123 us -> 0.04 us  [layer_backward(): shares = lax.psum_scatter(wide, 'dp', scatter_dimension=0, tiled=True)]
    all_to_all x4 -> x1, blocking collectives: 73.8 us -> 21.1 us  [across_chips(): lax.all_to_all(value, 'ctx', 0, 0, axis_index_groups=SAME_CORE, tiled=True)]
    ppermute x0 -> x42, starting transfers between devices: none -> 43.8 us  [the longest x36 40.6 us: ring(): return lambda value: lax.ppermute(value, axis, moves)]
    all_gather x1 -> x0, blocking collectives: 25.9 us -> none  [local(): lax.all_gather(vectors, 'dp', axis=0, tiled=False).transpose(1, 0, 2)]
    dot_general x24 -> x28, matrix products: 54.2 us -> 39.3 us  [dot(): lax.dot_general(left, right, (((ldim,), (rdim,)), ((), ())), preferred_el...]
    pallas_call x0 -> x6, Pallas kernels: none -> 14.8 us  [the longest x5 10.7 us: gather_end(): pl.pallas_call(join_kernel, in_specs=[pl.BlockSpec(memory_space=pltpu.SME...]
  transfers between devices with their start and end apart: 35 -> 70, of which waited for: 18 -> 33; matrix products, arithmetic and copies ran while one was open for 20% -> 19% of each run, Pallas kernels for 4% -> 6%
where the time goes in v2:
time: 548 us; the launch traced here: 537 us
  waiting for transfers between devices  182 us (33%)
  starting transfers between devices  108 us (20%)
  local copies, waits for them, and re-layouts  64.3 us (12%)
  Pallas kernels  45.8 us (8%)
  blocking collectives  43.2 us (8%)
  matrix products  39.3 us (7%)
  other arithmetic  37.9 us (7%)
  between operations  15.9 us (3%)
    ppermute x36, waiting for transfers between devices, ring(): return lambda value: lax.ppermute(value, axis, moves)  97.5 us
    ppermute x36, starting transfers between devices, ring(): return lambda value: lax.ppermute(value, axis, moves)  40.6 us
    dot_general x28, matrix products, dot(): lax.dot_general(left, right, (((ldim,), (rdim,)), ((), ())), preferred_el...  39.3 us
    all_to_all x3, waiting for transfers between devices, across_chips(): lax.all_to_all(value, 'ctx', 0, 0, axis_index_groups=SAME_CORE, tiled=True)  30.5 us
    ppermute x6, waiting for transfers between devices, across(): lax.ppermute(value, axis, [(i, (i + count // 2) % count) for i in range(c...  29.9 us
    ppermute x18, starting transfers between devices, swap(): return lax.ppermute(value, 'ctx', OTHER_CORE)  27.3 us
    all_to_all x1, blocking collectives, chip_sum(): lax.all_to_all(pieces, 'ctx', 0, 0, axis_index_groups=SAME_CORE, tiled=True)  22.1 us
    all_to_all x1, blocking collectives, across_chips(): lax.all_to_all(value, 'ctx', 0, 0, axis_index_groups=SAME_CORE, tiled=True)  21.1 us
  transfers between devices with their start and end apart: 70, of which 33 were waited for; matrix products, arithmetic and copies ran while one was open for 19% of the time, Pallas kernels for 6%

profile of v2, /device:TPU:1, one launch (start us, length us, event | category | flops | bytes accessed | tf_op | source)
XLA Modules:
  0.0 536.9 jit_solution(10741545983239686252)
XLA Ops:
  30.5 4.7 collective-permute-done.5.refs_7_
  61.9 21.1 %all_to_all.50.qkv_ref = bf16[8,192,256]{2,1,0:T(8,128)(2,1)S(1)} all-to-all(bf16[8,192,256]{2,1,0:T(8,128)(2,1)S(1)} %concatenate.66), channel_id=1, replica_groups={{0,2,4,6,8,10,12,14},{1,3,5,7,9,11,13,15},{16,18,20,22,24,26,28,30},{17..., dimensions={0} | all-to-all | bytes 1572864 | tf_op jit(solution)/shard_map/all_to_all | solution.py:244
  83.3 5.4 %attend.2 = (bf16[16,64,128]{2,1,0:T(8,128)(2,1)}, f32[8,64,256]{2,1,0:T(8,128)S(1)}, f32[8,1,256]{2,1,0:T(1,128)S(1)}) custom-call(bf16[8,192,256]{2,1,0:T(8,128)(2,1)S(1)} %all_to_all.50.qkv_ref), custom_call_target="tpu_custom_call" | custom-call | tf_op jit(solution)/shard_map/attend/pallas_call | solution.py:169
  91.0 14.1 %collective-permute-done.13.refs_7_ = bf16[1,96,4992]{2,1,0:T(8,128)(2,1)S(1)} collective-permute-done((bf16[1,96,4992]{2,1,0:T(8,128)(2,1)}, bf16[1,96,4992]{2,1,0:T(8,128)(2,1)S(1)}, u32[]{:S(2)}, u32[]{:S(2)}) %collective-permute-start.13) | collective-permute-done | bytes 958496 | tf_op jit(solution)/shard_map/ppermute | solution.py:45
  106.4 6.2 %all-to-all-start.1 = ((bf16[16,64,128]{2,1,0:T(8,128)(2,1)}), bf16[16,64,128]{2,1,0:T(8,128)(2,1)}, u32[]{:S(2)}, u32[]{:S(2)}) async-start(bf16[16,64,128]{2,1,0:T(8,128)(2,1)} %get-tuple-element.51), calls=%async_computation.1 | async-start | bytes 524288 | tf_op jit(solution)/shard_map/all_to_all | solution.py:260
  115.0 6.5 %all-to-all-done.1 = bf16[16,64,128]{2,1,0:T(8,128)(2,1)} async-done(((bf16[16,64,128]{2,1,0:T(8,128)(2,1)}), bf16[16,64,128]{2,1,0:T(8,128)(2,1)}, u32[]{:S(2)}, u32[]{:S(2)}) %all-to-all-start.1) | async-done | bytes 262176 | tf_op jit(solution)/shard_map/all_to_all | solution.py:260
  122.4 10.6 %collective-permute-done.11.refs_2_ = bf16[1,96,4992]{2,1,0:T(8,128)(2,1)} collective-permute-done((bf16[1,96,4992]{2,1,0:T(8,128)(2,1)}, bf16[1,96,4992]{2,1,0:T(8,128)(2,1)}, u32[]{:S(2)}, u32[]{:S(2)}) %collective-permute-start.11) | collective-permute-done | bytes 958496 | tf_op jit(solution)/shard_map/ppermute | solution.py:45
  133.0 6.2 %join.6 = bf16[8,96,4992]{2,1,0:T(8,128)(2,1)} custom-call(s32[8]{0:T(128)S(1)} %stack.143.where_ref, bf16[1,96,4992]{2,1,0:T(8,128)(2,1)S(1)} %bitcast.178, bf16[1,96,4992]{2,1,0:T(8,128)(2,1)} %collective-permute-done.9.refs_1_, bf16[1,96,4992]{2,1,0:T(8,128)(2,1)} %collective-permute-done.11.refs_2_, ...), custom_call_target="tpu_custom_call" | custom-call | tf_op jit(solution)/shard_map/join/pallas_call | solution.py:95
  168.2 9.5 %collective-permute-done.18.refs_4_ = bf16[1,96,3840]{2,1,0:T(8,128)(2,1)S(1)} collective-permute-done((bf16[1,96,3840]{2,1,0:T(8,128)(2,1)S(1)}, bf16[1,96,3840]{2,1,0:T(8,128)(2,1)S(1)}, u32[]{:S(2)}, u32[]{:S(2)}) %collective-permute-start.18) | collective-permute-done | bytes 737312 | tf_op jit(solution)/shard_map/ppermute | solution.py:50
  177.6 5.0 all-to-all-done.2.qkv_ref
  184.1 5.4 %attend.3 = (bf16[16,64,128]{2,1,0:T(8,128)(2,1)}, f32[8,64,256]{2,1,0:T(8,128)S(1)}, f32[8,1,256]{2,1,0:T(1,128)S(1)}) custom-call(bf16[8,192,256]{2,1,0:T(8,128)(2,1)S(1)} %all-to-all-done.2.qkv_ref), custom_call_target="tpu_custom_call" | custom-call | tf_op jit(solution)/shard_map/attend/pallas_call | solution.py:169
  190.4 9.5 %collective-permute-done.23.refs_7_ = bf16[1,96,3840]{2,1,0:T(8,128)(2,1)} collective-permute-done((bf16[1,96,3840]{2,1,0:T(8,128)(2,1)S(1)}, bf16[1,96,3840]{2,1,0:T(8,128)(2,1)}, u32[]{:S(2)}, u32[]{:S(2)}) %collective-permute-start.23) | collective-permute-done | bytes 737312 | tf_op jit(solution)/shard_map/ppermute | solution.py:45
  203.2 4.0 all-to-all-start.3
  210.9 5.1 all-to-all-done.3
  238.4 4.2 all-to-all-start.4
  244.8 5.7 %pad_maximum_fusion = bf16[768,3456]{1,0:T(8,128)(2,1)} fusion(bf16[768,384]{1,0:T(8,128)(2,1)S(1)} %add_convert_fusion.1, bf16[768,768]{1,0:T(8,128)(2,1)} %get-tuple-element.189, bf16[768,768]{1,0:T(8,128)(2,1)S(1)} %get-tuple-element.188, bf16[768,1536]{1,0:T(8,128)(2,1)S(1)} %copy-done.22), kind=kLoop, calls=%fused_computation.2 | loop fusion | flops 21233664 | bytes 10616832 | tf_op jit(solution)/shard_map/concatenate | solution.py:319
  251.5 10.1 %attend_back.2 = bf16[8,192,256]{2,1,0:T(8,128)(2,1)} custom-call(bf16[8,192,256]{2,1,0:T(8,128)(2,1)S(1)} %all-to-all-done.2.qkv_ref, bf16[16,64,128]{2,1,0:T(8,128)(2,1)S(1)} %all-to-all-done.4.grad_ref, f32[8,64,256]{2,1,0:T(8,128)S(1)} %copy-done.5, f32[8,1,256]{2,1,0:T(1,128)S(1)} %get-tuple-element.67.lse_ref), custom_call_target="tpu_custom_call" | custom-call | tf_op jit(solution)/shard_map/attend_back/pallas_call | solution.py:213
  261.6 6.6 %all-to-all-start.5 = ((bf16[8,192,256]{2,1,0:T(8,128)(2,1)}), bf16[8,192,256]{2,1,0:T(8,128)(2,1)S(1)}, u32[]{:S(2)}, u32[]{:S(2)}) async-start(bf16[8,192,256]{2,1,0:T(8,128)(2,1)} %attend_back.2), calls=%async_computation.5 | async-start | bytes 1572864 | tf_op jit(solution)/shard_map/all_to_all | solution.py:244
  271.8 11.0 %all-to-all-done.5 = bf16[8,192,256]{2,1,0:T(8,128)(2,1)S(1)} async-done(((bf16[8,192,256]{2,1,0:T(8,128)(2,1)}), bf16[8,192,256]{2,1,0:T(8,128)(2,1)S(1)}, u32[]{:S(2)}, u32[]{:S(2)}) %all-to-all-start.5) | async-done | bytes 786464 | tf_op jit(solution)/shard_map/all_to_all | solution.py:244
  334.9 10.1 %attend_back.3 = bf16[8,192,256]{2,1,0:T(8,128)(2,1)} custom-call(bf16[8,192,256]{2,1,0:T(8,128)(2,1)S(1)} %all_to_all.50.qkv_ref, bf16[16,64,128]{2,1,0:T(8,128)(2,1)S(1)} %all-to-all-done.6.grad_ref, f32[8,64,256]{2,1,0:T(8,128)S(1)} %copy-done.3, f32[8,1,256]{2,1,0:T(1,128)S(1)} %get-tuple-element.73.lse_ref), custom_call_target="tpu_custom_call" | custom-call | tf_op jit(solution)/shard_map/attend_back/pallas_call | solution.py:213
  345.0 4.4 all-to-all-done.7
  349.5 4.5 all-to-all-start.8
  354.1 14.5 %all-to-all-done.8 = bf16[8,192,256]{2,1,0:T(8,128)(2,1)} async-done(((bf16[8,192,256]{2,1,0:T(8,128)(2,1)}), bf16[8,192,256]{2,1,0:T(8,128)(2,1)}, u32[]{:S(2)}, u32[]{:S(2)}) %all-to-all-start.8) | async-done | bytes 786464 | tf_op jit(solution)/shard_map/all_to_all | solution.py:244
  389.5 27.5 %collective-permute-done.37 = bf16[96,2560]{1,0:T(8,128)(2,1)S(1)} collective-permute-done((bf16[96,2560]{1,0:T(8,128)(2,1)}, bf16[96,2560]{1,0:T(8,128)(2,1)S(1)}, u32[]{:S(2)}, u32[]{:S(2)}) %collective-permute-start.37) | collective-permute-done | bytes 491552 | tf_op jit(solution)/shard_map/ppermute | solution.py:45
  417.0 10.5 %collective-permute-done.39 = bf16[96,2560]{1,0:T(8,128)(2,1)S(1)} collective-permute-done((bf16[96,2560]{1,0:T(8,128)(2,1)S(1)}, bf16[96,2560]{1,0:T(8,128)(2,1)S(1)}, u32[]{:S(2)}, u32[]{:S(2)}) %collective-permute-start.39) | collective-permute-done | bytes 491552 | tf_op jit(solution)/shard_map/ppermute | solution.py:45
  430.8 10.8 %collective-permute-done.50 = bf16[96,2560]{1,0:T(8,128)(2,1)} collective-permute-done((bf16[96,2560]{1,0:T(8,128)(2,1)S(1)}, bf16[96,2560]{1,0:T(8,128)(2,1)}, u32[]{:S(2)}, u32[]{:S(2)}) %collective-permute-start.50) | collective-permute-done | bytes 491552 | tf_op jit(solution)/shard_map/ppermute | solution.py:45
  444.1 10.4 %collective-permute-done.51 = bf16[96,2560]{1,0:T(8,128)(2,1)S(1)} collective-permute-done((bf16[96,2560]{1,0:T(8,128)(2,1)S(1)}, bf16[96,2560]{1,0:T(8,128)(2,1)S(1)}, u32[]{:S(2)}, u32[]{:S(2)}) %collective-permute-start.51) | collective-permute-done | bytes 491552 | tf_op jit(solution)/shard_map/ppermute | solution.py:50
  457.2 22.1 %all_to_all.51 = bf16[8,96,768]{2,1,0:T(8,128)(2,1)S(1)} all-to-all(bf16[8,96,768]{2,1,0:T(8,128)(2,1)S(1)} %bitcast.204), channel_id=1, replica_groups={{0,2,4,6,8,10,12,14},{1,3,5,7,9,11,13,15},{16,18,20,22,24,26,28,30},{17..., dimensions={0} | all-to-all | bytes 2359296 | tf_op jit(solution)/shard_map/all_to_all | solution.py:362
  480.4 4.7 collective-permute-done.55.refs_4_
  495.2 6.9 %collective-permute-start.59 = (bf16[8,96,768]{2,1,0:T(8,128)(2,1)S(1)}, bf16[8,96,768]{2,1,0:T(8,128)(2,1)S(1)}, u32[]{:S(2)}, u32[]{:S(2)}) collective-permute-start(bf16[8,96,768]{2,1,0:T(8,128)(2,1)S(1)} %join.9.refs_2_), channel_id=1, source_target_pairs={{0,1},{1,0},{2,3},{3,2},{4,5},{5,4},{6,7},{7,6},{8,9},{9,8},{10,11... | collective-permute-start | bytes 3538952 | tf_op jit(solution)/shard_map/ppermute | solution.py:135
  502.6 5.3 collective-permute-done.44.refs_4_
  523.9 4.1 unpack.1
  (511 shorter events, 234.3 us)
Async XLA Ops:
  12.4 18.0 %collective-permute-start = (bf16[1,112,1152]{2,1,0:T(8,128)(2,1)S(1)}, bf16[1,112,1152]{2,1,0:T(8,128)(2,1)S(1)}, u32[]{:S(2)}, u32[]{:S(2)}) collective-permute-start(bf16[1,112,1152]{2,1,0:T(8,128)(2,1)S(1)} %fusion.86.refs_0_), channel_id=1, source_target_pairs={{0,16},{16,32},{32,48},{48,0},{64,80},{80,96},{96,112},{112,64},{1... | collective-permute-start | bytes 774152 | tf_op jit(solution)/shard_map/ppermute | solution.py:45
  14.9 26.8 %collective-permute-start.2 = (bf16[1,112,1152]{2,1,0:T(8,128)(2,1)S(1)}, bf16[1,112,1152]{2,1,0:T(8,128)(2,1)S(1)}, u32[]{:S(2)}, u32[]{:S(2)}) collective-permute-start(bf16[1,112,1152]{2,1,0:T(8,128)(2,1)S(1)} %fusion.86.refs_0_), channel_id=1, source_target_pairs={{0,48},{16,0},{32,16},{48,32},{64,112},{80,64},{96,80},{112,96},{1... | collective-permute-start | bytes 774152 | tf_op jit(solution)/shard_map/ppermute | solution.py:45
  30.2 13.4 %collective-permute-start.4 = (bf16[1,112,1152]{2,1,0:T(8,128)(2,1)S(1)}, bf16[1,112,1152]{2,1,0:T(8,128)(2,1)S(1)}, u32[]{:S(2)}, u32[]{:S(2)}) collective-permute-start(bf16[1,112,1152]{2,1,0:T(8,128)(2,1)S(1)} %collective-permute-done.3.refs_4_), channel_id=1, source_target_pairs={{0,16},{16,32},{32,48},{48,0},{64,80},{80,96},{96,112},{112,64},{1... | collective-permute-start | bytes 774152 | tf_op jit(solution)/shard_map/ppermute | solution.py:45
  50.5 32.5 %collective-permute-start.8 = (bf16[1,96,4992]{2,1,0:T(8,128)(2,1)S(1)}, bf16[1,96,4992]{2,1,0:T(8,128)(2,1)}, u32[]{:S(2)}, u32[]{:S(2)}) collective-permute-start(bf16[1,96,4992]{2,1,0:T(8,128)(2,1)S(1)} %bitcast.175), channel_id=1, source_target_pairs={{0,64},{16,80},{32,96},{48,112},{64,0},{80,16},{96,32},{112,48},{1... | collective-permute-start | bytes 2875400 | tf_op jit(solution)/shard_map/ppermute | solution.py:50
  50.8 32.3 %collective-permute-start.9 = (bf16[1,96,4992]{2,1,0:T(8,128)(2,1)S(1)}, bf16[1,96,4992]{2,1,0:T(8,128)(2,1)}, u32[]{:S(2)}, u32[]{:S(2)}) collective-permute-start(bf16[1,96,4992]{2,1,0:T(8,128)(2,1)S(1)} %bitcast.176), channel_id=1, source_target_pairs={{0,16},{16,32},{32,48},{48,0},{64,80},{80,96},{96,112},{112,64},{1... | collective-permute-start | bytes 2875400 | tf_op jit(solution)/shard_map/ppermute | solution.py:45
  50.8 32.3 %collective-permute-start.10 = (bf16[1,96,4992]{2,1,0:T(8,128)(2,1)S(1)}, bf16[1,96,4992]{2,1,0:T(8,128)(2,1)}, u32[]{:S(2)}, u32[]{:S(2)}) collective-permute-start(bf16[1,96,4992]{2,1,0:T(8,128)(2,1)S(1)} %bitcast.177), channel_id=1, source_target_pairs={{0,48},{16,0},{32,16},{48,32},{64,112},{80,64},{96,80},{112,96},{1... | collective-permute-start | bytes 2875400 | tf_op jit(solution)/shard_map/ppermute | solution.py:45
  83.1 22.0 %collective-permute-start.13 = (bf16[1,96,4992]{2,1,0:T(8,128)(2,1)}, bf16[1,96,4992]{2,1,0:T(8,128)(2,1)S(1)}, u32[]{:S(2)}, u32[]{:S(2)}) collective-permute-start(bf16[1,96,4992]{2,1,0:T(8,128)(2,1)} %collective-permute-done.8.refs_4_), channel_id=1, source_target_pairs={{0,48},{16,0},{32,16},{48,32},{64,112},{80,64},{96,80},{112,96},{1... | collective-permute-start | bytes 2875400 | tf_op jit(solution)/shard_map/ppermute | solution.py:45
  89.6 43.5 %collective-permute-start.12 = (bf16[1,96,4992]{2,1,0:T(8,128)(2,1)}, bf16[1,96,4992]{2,1,0:T(8,128)(2,1)}, u32[]{:S(2)}, u32[]{:S(2)}) collective-permute-start(bf16[1,96,4992]{2,1,0:T(8,128)(2,1)} %collective-permute-done.8.refs_4_), channel_id=1, source_target_pairs={{0,16},{16,32},{32,48},{48,0},{64,80},{80,96},{96,112},{112,64},{1... | collective-permute-start | bytes 2875400 | tf_op jit(solution)/shard_map/ppermute | solution.py:45
  91.0 42.0 %collective-permute-start.11 = (bf16[1,96,4992]{2,1,0:T(8,128)(2,1)}, bf16[1,96,4992]{2,1,0:T(8,128)(2,1)}, u32[]{:S(2)}, u32[]{:S(2)}) collective-permute-start(bf16[1,96,4992]{2,1,0:T(8,128)(2,1)} %collective-permute-done.9.refs_1_), channel_id=1, source_target_pairs={{0,16},{16,32},{32,48},{48,0},{64,80},{80,96},{96,112},{112,64},{1... | collective-permute-start | bytes 2875400 | tf_op jit(solution)/shard_map/ppermute | solution.py:45
  105.1 27.9 %collective-permute-start.14 = (bf16[1,96,4992]{2,1,0:T(8,128)(2,1)S(1)}, bf16[1,96,4992]{2,1,0:T(8,128)(2,1)}, u32[]{:S(2)}, u32[]{:S(2)}) collective-permute-start(bf16[1,96,4992]{2,1,0:T(8,128)(2,1)S(1)} %collective-permute-done.13.refs_7_), channel_id=1, source_target_pairs={{0,48},{16,0},{32,16},{48,32},{64,112},{80,64},{96,80},{112,96},{1... | collective-permute-start | bytes 2875400 | tf_op jit(solution)/shard_map/ppermute | solution.py:45
  106.4 15.0 %all-to-all-start.1 = ((bf16[16,64,128]{2,1,0:T(8,128)(2,1)}), bf16[16,64,128]{2,1,0:T(8,128)(2,1)}, u32[]{:S(2)}, u32[]{:S(2)}) async-start(bf16[16,64,128]{2,1,0:T(8,128)(2,1)} %get-tuple-element.51), calls=%async_computation.1 | async-start | bytes 524288 | tf_op jit(solution)/shard_map/all_to_all | solution.py:260
  156.1 21.5 %collective-permute-start.18 = (bf16[1,96,3840]{2,1,0:T(8,128)(2,1)S(1)}, bf16[1,96,3840]{2,1,0:T(8,128)(2,1)S(1)}, u32[]{:S(2)}, u32[]{:S(2)}) collective-permute-start(bf16[1,96,3840]{2,1,0:T(8,128)(2,1)S(1)} %bitcast.169), channel_id=1, source_target_pairs={{0,64},{16,80},{32,96},{48,112},{64,0},{80,16},{96,32},{112,48},{1... | collective-permute-start | bytes 2211848 | tf_op jit(solution)/shard_map/ppermute | solution.py:50
  156.6 21.1 %collective-permute-start.19 = (bf16[1,96,3840]{2,1,0:T(8,128)(2,1)S(1)}, bf16[1,96,3840]{2,1,0:T(8,128)(2,1)}, u32[]{:S(2)}, u32[]{:S(2)}) collective-permute-start(bf16[1,96,3840]{2,1,0:T(8,128)(2,1)S(1)} %bitcast.170), channel_id=1, source_target_pairs={{0,16},{16,32},{32,48},{48,0},{64,80},{80,96},{96,112},{112,64},{1... | collective-permute-start | bytes 2211848 | tf_op jit(solution)/shard_map/ppermute | solution.py:45
  156.8 20.8 %collective-permute-start.20 = (bf16[1,96,3840]{2,1,0:T(8,128)(2,1)S(1)}, bf16[1,96,3840]{2,1,0:T(8,128)(2,1)}, u32[]{:S(2)}, u32[]{:S(2)}) collective-permute-start(bf16[1,96,3840]{2,1,0:T(8,128)(2,1)S(1)} %bitcast.171), channel_id=1, source_target_pairs={{0,48},{16,0},{32,16},{48,32},{64,112},{80,64},{96,80},{112,96},{1... | collective-permute-start | bytes 2211848 | tf_op jit(solution)/shard_map/ppermute | solution.py:45
  164.5 18.1 %all-to-all-start.2 = ((bf16[8,192,256]{2,1,0:T(8,128)(2,1)}), bf16[8,192,256]{2,1,0:T(8,128)(2,1)S(1)}, u32[]{:S(2)}, u32[]{:S(2)}) async-start(bf16[8,192,256]{2,1,0:T(8,128)(2,1)} %concatenate.70), calls=%async_computation.2 | async-start | bytes 1572864 | tf_op jit(solution)/shard_map/all_to_all | solution.py:244
  182.6 17.3 %collective-permute-start.23 = (bf16[1,96,3840]{2,1,0:T(8,128)(2,1)S(1)}, bf16[1,96,3840]{2,1,0:T(8,128)(2,1)}, u32[]{:S(2)}, u32[]{:S(2)}) collective-permute-start(bf16[1,96,3840]{2,1,0:T(8,128)(2,1)S(1)} %collective-permute-done.18.refs_4_), channel_id=1, source_target_pairs={{0,48},{16,0},{32,16},{48,32},{64,112},{80,64},{96,80},{112,96},{1... | collective-permute-start | bytes 2211848 | tf_op jit(solution)/shard_map/ppermute | solution.py:45
  182.7 34.0 %collective-permute-start.22 = (bf16[1,96,3840]{2,1,0:T(8,128)(2,1)S(1)}, bf16[1,96,3840]{2,1,0:T(8,128)(2,1)}, u32[]{:S(2)}, u32[]{:S(2)}) collective-permute-start(bf16[1,96,3840]{2,1,0:T(8,128)(2,1)S(1)} %collective-permute-done.18.refs_4_), channel_id=1, source_target_pairs={{0,16},{16,32},{32,48},{48,0},{64,80},{80,96},{96,112},{112,64},{1... | collective-permute-start | bytes 2211848 | tf_op jit(solution)/shard_map/ppermute | solution.py:45
  184.1 32.6 %collective-permute-start.21 = (bf16[1,96,3840]{2,1,0:T(8,128)(2,1)}, bf16[1,96,3840]{2,1,0:T(8,128)(2,1)}, u32[]{:S(2)}, u32[]{:S(2)}) collective-permute-start(bf16[1,96,3840]{2,1,0:T(8,128)(2,1)} %collective-permute-done.19.refs_1_), channel_id=1, source_target_pairs={{0,16},{16,32},{32,48},{48,0},{64,80},{80,96},{96,112},{112,64},{1... | collective-permute-start | bytes 2211848 | tf_op jit(solution)/shard_map/ppermute | solution.py:45
  199.9 16.8 %collective-permute-start.24 = (bf16[1,96,3840]{2,1,0:T(8,128)(2,1)}, bf16[1,96,3840]{2,1,0:T(8,128)(2,1)}, u32[]{:S(2)}, u32[]{:S(2)}) collective-permute-start(bf16[1,96,3840]{2,1,0:T(8,128)(2,1)} %collective-permute-done.23.refs_7_), channel_id=1, source_target_pairs={{0,48},{16,0},{32,16},{48,32},{64,112},{80,64},{96,80},{112,96},{1... | collective-permute-start | bytes 2211848 | tf_op jit(solution)/shard_map/ppermute | solution.py:45
  203.2 12.7 %all-to-all-start.3 = ((bf16[16,64,128]{2,1,0:T(8,128)(2,1)}), bf16[16,64,128]{2,1,0:T(8,128)(2,1)S(1)}, u32[]{:S(2)}, u32[]{:S(2)}) async-start(bf16[16,64,128]{2,1,0:T(8,128)(2,1)} %get-tuple-element.58), calls=%async_computation.3 | async-start | bytes 524288 | tf_op jit(solution)/shard_map/all_to_all | solution.py:260
  238.4 12.9 %all-to-all-start.4 = ((bf16[16,64,128]{2,1,0:T(8,128)(2,1)}), bf16[16,64,128]{2,1,0:T(8,128)(2,1)S(1)}, u32[]{:S(2)}, u32[]{:S(2)}) async-start(bf16[16,64,128]{2,1,0:T(8,128)(2,1)} %concatenate.75), calls=%async_computation.4 | async-start | bytes 524288 | tf_op jit(solution)/shard_map/all_to_all | solution.py:313
  242.6 86.2 %reduce-scatter.3.cloned.1.call-start = ((), (), s32[]{:S(2)}) async-start(), calls=%async_computation.12 | async-start | bytes 5971968 | tf_op jit(solution)/shard_map/reduce_scatter | solution.py:321
  261.6 21.1 %all-to-all-start.5 = ((bf16[8,192,256]{2,1,0:T(8,128)(2,1)}), bf16[8,192,256]{2,1,0:T(8,128)(2,1)S(1)}, u32[]{:S(2)}, u32[]{:S(2)}) async-start(bf16[8,192,256]{2,1,0:T(8,128)(2,1)} %attend_back.2), calls=%async_computation.5 | async-start | bytes 1572864 | tf_op jit(solution)/shard_map/all_to_all | solution.py:244
  320.0 135.9 %reduce-scatter.5.cloned.1.call-start = ((), (), s32[]{:S(2)}) async-start(), calls=%async_computation.13 | async-start | bytes 5971968 | tf_op jit(solution)/shard_map/reduce_scatter | solution.py:321
  330.9 18.5 %all-to-all-start.7 = ((bf16[8,96,512]{2,1,0:T(8,128)(2,1)}), bf16[8,96,512]{2,1,0:T(8,128)(2,1)S(1)}, u32[]{:S(2)}, u32[]{:S(2)}) async-start(bf16[8,96,512]{2,1,0:T(8,128)(2,1)} %bitcast.154), calls=%async_computation.8 | async-start | bytes 1572864 | tf_op jit(solution)/shard_map/all_to_all | solution.py:362
  349.5 19.1 %all-to-all-start.8 = ((bf16[8,192,256]{2,1,0:T(8,128)(2,1)}), bf16[8,192,256]{2,1,0:T(8,128)(2,1)}, u32[]{:S(2)}, u32[]{:S(2)}) async-start(bf16[8,192,256]{2,1,0:T(8,128)(2,1)} %attend_back.3), calls=%async_computation.9 | async-start | bytes 1572864 | tf_op jit(solution)/shard_map/all_to_all | solution.py:244
  383.9 33.1 %collective-permute-start.37 = (bf16[96,2560]{1,0:T(8,128)(2,1)}, bf16[96,2560]{1,0:T(8,128)(2,1)S(1)}, u32[]{:S(2)}, u32[]{:S(2)}) collective-permute-start(bf16[96,2560]{1,0:T(8,128)(2,1)} %get-tuple-element.185), channel_id=1, source_target_pairs={{0,16},{16,32},{32,48},{48,0},{64,80},{80,96},{96,112},{112,64},{1... | collective-permute-start | bytes 1474568 | tf_op jit(solution)/shard_map/ppermute | solution.py:45
  383.9 33.1 %collective-permute-start.38 = (bf16[96,2560]{1,0:T(8,128)(2,1)}, bf16[96,2560]{1,0:T(8,128)(2,1)}, u32[]{:S(2)}, u32[]{:S(2)}) collective-permute-start(bf16[96,2560]{1,0:T(8,128)(2,1)} %get-tuple-element.184), channel_id=1, source_target_pairs={{0,48},{16,0},{32,16},{48,32},{64,112},{80,64},{96,80},{112,96},{1... | collective-permute-start | bytes 1474568 | tf_op jit(solution)/shard_map/ppermute | solution.py:45
  386.8 40.7 %collective-permute-start.39 = (bf16[96,2560]{1,0:T(8,128)(2,1)S(1)}, bf16[96,2560]{1,0:T(8,128)(2,1)S(1)}, u32[]{:S(2)}, u32[]{:S(2)}) collective-permute-start(bf16[96,2560]{1,0:T(8,128)(2,1)S(1)} %get-tuple-element.183), channel_id=1, source_target_pairs={{0,16},{16,32},{32,48},{48,0},{64,80},{80,96},{96,112},{112,64},{1... | collective-permute-start | bytes 1474568 | tf_op jit(solution)/shard_map/ppermute | solution.py:45
  386.8 40.7 %collective-permute-start.40 = (bf16[96,2560]{1,0:T(8,128)(2,1)S(1)}, bf16[96,2560]{1,0:T(8,128)(2,1)S(1)}, u32[]{:S(2)}, u32[]{:S(2)}) collective-permute-start(bf16[96,2560]{1,0:T(8,128)(2,1)S(1)} %get-tuple-element.182), channel_id=1, source_target_pairs={{0,48},{16,0},{32,16},{48,32},{64,112},{80,64},{96,80},{112,96},{1... | collective-permute-start | bytes 1474568 | tf_op jit(solution)/shard_map/ppermute | solution.py:45
  429.2 14.1 %collective-permute-start.49 = (bf16[96,2560]{1,0:T(8,128)(2,1)S(1)}, bf16[96,2560]{1,0:T(8,128)(2,1)S(1)}, u32[]{:S(2)}, u32[]{:S(2)}) collective-permute-start(bf16[96,2560]{1,0:T(8,128)(2,1)S(1)} %get-tuple-element.180), channel_id=1, source_target_pairs={{0,16},{16,32},{32,48},{48,0},{64,80},{80,96},{96,112},{112,64},{1... | collective-permute-start | bytes 1474568 | tf_op jit(solution)/shard_map/ppermute | solution.py:45
  495.2 28.7 %collective-permute-start.59 = (bf16[8,96,768]{2,1,0:T(8,128)(2,1)S(1)}, bf16[8,96,768]{2,1,0:T(8,128)(2,1)S(1)}, u32[]{:S(2)}, u32[]{:S(2)}) collective-permute-start(bf16[8,96,768]{2,1,0:T(8,128)(2,1)S(1)} %join.9.refs_2_), channel_id=1, source_target_pairs={{0,1},{1,0},{2,3},{3,2},{4,5},{5,4},{6,7},{7,6},{8,9},{9,8},{10,11... | collective-permute-start | bytes 3538952 | tf_op jit(solution)/shard_map/ppermute | solution.py:135
  (123 other events, 879.3 us)
Sparse Core Ops, SparseCore 0:
  251.4 72.9 reduce-scatter.2
  328.9 90.8 reduce-scatter.4
